TPU v7x, 768 devices: a whole 4x8x12 slice. The times are simulated.
768 devices in a mesh: grp: 12 (over z), blk: 8 (over x, core), sub: 8 (over y).
Axes of the slice: x: 4, y: 8, z: 12, core: 2. Of those that a mesh axis runs over, the one named last changes fastest.
Arguments:
- mass_per_volume: float32 [32, 256, 1536], P('blk', 'sub', 'grp'), may hold values from 0.8 to 1.2
- flow_speed_vector: float32 [3, 32, 256, 1536], P(None, 'blk', 'sub', 'grp'), may hold values from -1 to 1
- normal_stress: float32 [32, 256, 1536], P('blk', 'sub', 'grp'), may hold values from 0.8 to 1.2
- facing_strip_index: int32 [12, 8, 256], P('grp', 'blk', 'sub'), may hold values from 0 to 511, as said below
- solid_kelvin: float32 [64, 64, 1536], P('blk', 'sub', 'grp'), may hold values from 0.5 to 1.5
- face_coupling: float32 [6, 64, 64, 1536], P(None, 'blk', 'sub', 'grp'), may hold values from 0 to 2, as said below
- substance_index: int32 [64, 64, 1536], P('blk', 'sub', 'grp'), may hold values from 0 to 7
- substance_storage: float32 [8], replicated, may hold values from 0.5 to 4
Outputs:
- fluid_next: float32 [5, 32, 256, 1536], P(None, 'blk', 'sub', 'grp')
- metal_next: float32 [64, 64, 1536], P('blk', 'sub', 'grp')
Inputs may be any that keep to these rules, and one draw needn't show every extreme that they name: `facing_strip_index`: A value v names metal device v // 8 of the blade (devices numbered over blk then sub) and strip v % 8 on it. The strips of each fluid device name exactly 32 distinct metal devices, each exactly 1 times; strips within a metal device are named with any multiplicity. `face_coupling`: channels 0 to 2 are the conductances across the lower x, y and z face of each cell, channels 3 to 5 across the upper ones; a cell's upper conductance equals the lower one of the next cell along that dimension. Conductances across the grid's ends in x and y and across multiples of 128 along z are zero, all others lie in 0.2 to 2.
All inputs are finite; a program needn't handle non-finite values.
Results may differ from a plain program's by a relative error of at most 0.0001.
Values sent between devices are 32-bit elements; how exact they have to be, the bound alone decides.
A program may use at most 32 MiB of HBM per device.

v0:
```python
import jax
import jax.numpy as jnp
from jax import lax
from jax.sharding import PartitionSpec as P

ITERS = 4


gamma_gas = 1.4
time_step = 0.1
viscosity = 0.05
film_coeff = 1.0
third_part = 1.0 / 3.0
two_thirds = 2.0 / 3.0


def extended(block, sides, width, periodic):
    for axis, dim in sides:
        count = lax.axis_size(axis)
        forward = [(i, i + 1) for i in range(count - 1)]
        if periodic:
            forward.append((count - 1, 0))
        backward = [(target, source) for source, target in forward]
        low = lax.ppermute(
            lax.slice_in_dim(block, block.shape[dim] - width, None, axis=dim), axis, forward
        )
        high = lax.ppermute(lax.slice_in_dim(block, 0, width, axis=dim), axis, backward)
        block = jnp.concatenate([low, block, high], axis=dim)
    return block


def cut_faces(values, axis_id, start_at, stop_at):
    first_space = values.ndim - 3
    indexer = [slice(None)] * values.ndim
    for member in range(3):
        if member == axis_id:
            indexer[first_space + member] = slice(start_at, stop_at)
        else:
            indexer[first_space + member] = slice(1, -1)
    return values[tuple(indexer)]


def cut_along(values, axis_id, start_at, stop_at):
    indexer = [slice(None)] * values.ndim
    indexer[values.ndim - 3 + axis_id] = slice(start_at, stop_at)
    return values[tuple(indexer)]


def crop_cells(values, margin):
    return values[..., margin:-margin, margin:-margin, margin:-margin]


def advance_rate(padded, source):
    mass_per_volume = padded[0]
    flow_speed_vector = padded[1:4] / mass_per_volume
    kinetic = 0.5 * jnp.sum(padded[1:4] * flow_speed_vector, axis=0)
    normal_stress = (gamma_gas - 1.0) * (padded[4] - kinetic)
    sound_speed = jnp.sqrt(gamma_gas * normal_stress / mass_per_volume)
    interior = crop_cells(padded, 1)
    rate_sum = jnp.zeros_like(interior)
    smooth_sum = jnp.zeros_like(interior)
    for axis_id in range(3):
        along_vel = flow_speed_vector[axis_id]
        flux_dir = padded * along_vel
        flux_dir = flux_dir.at[1 + axis_id].add(normal_stress)
        flux_dir = flux_dir.at[4].add(normal_stress * along_vel)
        wave_speed = jnp.abs(along_vel) + sound_speed
        left_flux = cut_faces(flux_dir, axis_id, 0, -1)
        right_flux = cut_faces(flux_dir, axis_id, 1, None)
        left_state = cut_faces(padded, axis_id, 0, -1)
        right_state = cut_faces(padded, axis_id, 1, None)
        face_speed = jnp.maximum(
            cut_faces(wave_speed, axis_id, 0, -1), cut_faces(wave_speed, axis_id, 1, None)
        )
        face_flux = 0.5 * (left_flux + right_flux) - 0.5 * face_speed * (right_state - left_state)
        rate_sum = rate_sum - (
            cut_along(face_flux, axis_id, 1, None) - cut_along(face_flux, axis_id, 0, -1)
        )
        line_cut = cut_faces(padded, axis_id, None, None)
        smooth_sum = smooth_sum + (
            cut_along(line_cut, axis_id, 2, None)
            - 2.0 * cut_along(line_cut, axis_id, 1, -1)
            + cut_along(line_cut, axis_id, 0, -2)
        )
    weights = jnp.array([0.0, 1.0, 1.0, 1.0, 1.0], jnp.float32).reshape(5, 1, 1, 1)
    rate_sum = rate_sum + viscosity * weights * smooth_sum
    return rate_sum.at[4].add(-source)


def fluid_state(mass_per_volume, flow_speed_vector, normal_stress):
    momentum = mass_per_volume[None] * flow_speed_vector
    energy = normal_stress / (gamma_gas - 1.0) + 0.5 * jnp.sum(momentum * flow_speed_vector, axis=0)
    return jnp.concatenate([mass_per_volume[None], momentum, energy[None]], axis=0)


def section_update(section_no, base, present_iterate, source):
    fresh = crop_cells(present_iterate, 1) + time_step * advance_rate(present_iterate, source)
    if section_no == 0:
        return fresh
    if section_no == 1:
        return 0.75 * base + 0.25 * fresh
    return third_part * base + two_thirds * fresh


def metal_apply(padded, face_coupling, storage_coefficient):
    center = padded[1:-1, 1:-1, 1:-1]
    result = storage_coefficient * center
    result = (
        result
        + face_coupling[0] * (center - padded[:-2, 1:-1, 1:-1])
        + face_coupling[3] * (center - padded[2:, 1:-1, 1:-1])
    )
    result = (
        result
        + face_coupling[1] * (center - padded[1:-1, :-2, 1:-1])
        + face_coupling[4] * (center - padded[1:-1, 2:, 1:-1])
    )
    result = (
        result
        + face_coupling[2] * (center - padded[1:-1, 1:-1, :-2])
        + face_coupling[5] * (center - padded[1:-1, 1:-1, 2:])
    )
    return result


def solid_conduction_apply(field_in, face_coupling, storage_coefficient):
    padded = extended(field_in, (("blk", 0), ("sub", 1)), 1, False)
    padded = jnp.pad(padded, ((0, 0), (0, 0), (1, 1)))
    return metal_apply(padded, face_coupling, storage_coefficient)


def squared_sum(equation_misfit):
    return lax.psum(jnp.sum(equation_misfit * equation_misfit), ("blk", "sub"))


def shards(
    mass_per_volume,
    flow_speed_vector,
    normal_stress,
    facing_strip_index,
    solid_kelvin,
    face_coupling,
    substance_index,
    substance_storage,
):
    highest = lax.Precision.HIGHEST
    fy_cells = mass_per_volume.shape[1]
    solid_across_count = solid_kelvin.shape[1]
    conserved = fluid_state(mass_per_volume, flow_speed_vector, normal_stress)
    face_temp = normal_stress[0] / mass_per_volume[0]
    surface_kelvin = solid_kelvin[0]
    routes = facing_strip_index.reshape(fy_cells)
    every_surface = lax.all_gather(surface_kelvin, ("blk", "sub"), axis=0, tiled=True)
    wall_seen = jnp.take(every_surface, routes, axis=0)
    heat_flux = film_coeff * (face_temp - wall_seen)
    columns = lax.iota(jnp.int32, solid_across_count * lax.axis_size(("blk", "sub")))
    matches = (routes[:, None] == columns[None, :]).astype(jnp.float32)
    arriving_energy = lax.psum_scatter(
        jnp.dot(matches.T, heat_flux, precision=highest),
        ("blk", "sub"),
        scatter_dimension=0,
        tiled=True,
    )
    sink = jnp.zeros_like(mass_per_volume).at[0].set(heat_flux)
    present_iterate = conserved
    for section_no in range(3):
        padded = extended(present_iterate, (("grp", 3), ("blk", 1), ("sub", 2)), 1, True)
        present_iterate = section_update(section_no, conserved, padded, sink)
    mats_count = substance_storage.shape[0]
    storage_coefficient = jnp.sum(
        jnp.where(
            substance_index[None] == lax.iota(jnp.int32, mats_count)[:, None, None, None],
            substance_storage[:, None, None, None],
            0.0,
        ),
        axis=0,
    )
    kelvin_distribution = jnp.zeros_like(solid_kelvin).at[0].set(arriving_energy)
    forcing_vector = storage_coefficient * solid_kelvin + kelvin_distribution
    converged_kelvin = solid_kelvin
    equation_misfit = forcing_vector - solid_conduction_apply(
        converged_kelvin, face_coupling, storage_coefficient
    )
    search_vector = equation_misfit
    norm_now = squared_sum(equation_misfit)
    for step_no in range(ITERS):
        image_dir = solid_conduction_apply(search_vector, face_coupling, storage_coefficient)
        search_factor = norm_now / lax.psum(jnp.sum(search_vector * image_dir), ("blk", "sub"))
        converged_kelvin = converged_kelvin + search_factor * search_vector
        equation_misfit = equation_misfit - search_factor * image_dir
        norm_next = squared_sum(equation_misfit)
        search_vector = equation_misfit + norm_next / norm_now * search_vector
        norm_now = norm_next
    return (present_iterate, converged_kelvin)


def solution(mesh):
    in_specs = (
        P("blk", "sub", "grp"),
        P(None, "blk", "sub", "grp"),
        P("blk", "sub", "grp"),
        P("grp", "blk", "sub"),
        P("blk", "sub", "grp"),
        P(None, "blk", "sub", "grp"),
        P("blk", "sub", "grp"),
        P(),
    )
    out_specs = (P(None, "blk", "sub", "grp"), P("blk", "sub", "grp"))
    return jax.shard_map(shards, mesh=mesh, in_specs=in_specs, out_specs=out_specs, check_vma=False)
```

profile of v0, /device:TPU:1, one launch (start us, length us, event | category | flops | bytes accessed | tf_op | source)
XLA Modules:
  0.0 1283.7 jit_solution(6160504999455028293)
XLA Ops:
  7.2 1.0 broadcast_multiply_fusion.9
  8.2 0.9 add_bitcast_fusion
  9.1 0.9 pad_maximum_fusion.32
  10.2 15.1 %collective-permute-start.1 = (f32[5,4,32,1]{3,2,1,0:T(8,128)S(1)}, f32[5,4,32,1]{3,2,1,0:T(8,128)S(1)}, u32[]{:S(2)}, u32[]{:S(2)}) collective-permute-start(f32[5,4,32,1]{3,2,1,0:T(8,128)S(1)} %get-tuple-element.367), channel_id=1, source_target_pairs={{64,0},{128,64},{192,128},{256,192},{320,256},{384,320},{448,384},... | collective-permute-start | bytes 7688 | tf_op jit(solution)/shard_map/ppermute | solution.py:27
  25.3 1.9 collective-permute-start
  27.3 4.0 collective-permute-start.18
  31.2 1.9 collective-permute-start.19
  33.2 44.5 %all-gather = f32[1,512,128]{2,1,0:T(8,128)S(1)} all-gather(f32[1,8,128]{2,1,0:T(8,128)S(1)} %get-tuple-element.398), channel_id=2, replica_groups=mesh['grp'=12,'blk'=8,'sub'=8] {'blk','sub'}, dimensions={1}, use_global_device_ids=true | all-gather | bytes 266240 | tf_op jit(solution)/shard_map/all_gather | solution.py:153
  78.3 1.2 fusion.106
  80.3 1.3 dynamic-slice.175
  82.9 1.3 collective-permute-start.21
  84.2 4.0 collective-permute-start.20
  88.4 1.5 collective-permute-start.3
  91.6 1.5 collective-permute-done.3
  93.4 1.9 collective-permute-start.5
  95.3 3.4 collective-permute-start.4
  98.7 1.7 pad_maximum_fusion.4
  101.8 0.9 abs_add_fusion.8
  103.9 1.1 copy-done.1
  105.0 1.7 fusion.9
  106.7 165.7 %all-reduce.10.cloned.1.call-done = f32[512,128]{1,0:T(8,128)} async-done(((f32[512,128]{1,0:T(8,128)}), f32[512,128]{1,0:T(8,128)}) %all-reduce.10.cloned.1.call-update) | async-done | bytes 262160
  273.1 1.1 fusion.175
  274.2 1.9 collective-permute-start.23
  276.1 3.6 collective-permute-start.22
  280.6 1.3 collective-permute-start.25
  281.9 4.0 collective-permute-start.24
  285.9 2.1 pad_maximum_fusion.1
  288.8 116.6 %all-reduce.7 = (f32[]{:T(128)}, f32[]{:T(128)}) all-reduce(f32[]{:T(128)} %get-tuple-element.279, f32[]{:T(128)} %get-tuple-element.278), channel_id=1, replica_groups=mesh['grp'=12,'blk'=8,'sub'=8] {'blk','sub'}, use_global_device_ids=true, to_apply=%region_7.8 | all-reduce | flops 2 | bytes 16 | tf_op jit(solution)/shard_map/psum | solution.py:133
  407.4 1.9 fusion.23
  409.3 125.6 %psum.58 = f32[]{:T(128)} all-reduce(f32[]{:T(128)} %multiply_reduce_fusion.8), channel_id=1, replica_groups=mesh['grp'=12,'blk'=8,'sub'=8] {'blk','sub'}, use_global_device_ids=true, to_apply=%region_11.12 | all-reduce | flops 1 | bytes 8 | tf_op jit(solution)/shard_map/psum | solution.py:133
  536.3 10.9 collective-permute-start.27
  547.2 1.9 collective-permute-start.26
  549.3 1.0 collective-permute-done.26
  550.3 1.3 collective-permute-start.29
  551.6 4.0 collective-permute-start.28
  555.6 2.5 fusion.26
  559.0 117.8 %psum.59 = f32[]{:T(128)} all-reduce(f32[]{:T(128)} %get-tuple-element.286), channel_id=1, replica_groups=mesh['grp'=12,'blk'=8,'sub'=8] {'blk','sub'}, use_global_device_ids=true, to_apply=%region_13.14 | all-reduce | flops 1 | bytes 8 | tf_op jit(solution)/shard_map/psum | solution.py:188
  678.8 125.5 %psum.60 = f32[]{:T(128)} all-reduce(f32[]{:T(128)} %get-tuple-element.284), channel_id=1, replica_groups=mesh['grp'=12,'blk'=8,'sub'=8] {'blk','sub'}, use_global_device_ids=true, to_apply=%region_15.16 | all-reduce | flops 1 | bytes 8 | tf_op jit(solution)/shard_map/psum | solution.py:133
  805.7 10.9 collective-permute-start.31
  816.6 1.9 collective-permute-start.30
  818.5 2.5 fusion.58
  821.1 1.3 collective-permute-start.33
  822.4 4.0 collective-permute-start.32
  827.9 119.6 %psum.61 = f32[]{:T(128)} all-reduce(f32[]{:T(128)} %get-tuple-element.282), channel_id=1, replica_groups=mesh['grp'=12,'blk'=8,'sub'=8] {'blk','sub'}, use_global_device_ids=true, to_apply=%region_17.18 | all-reduce | flops 1 | bytes 8 | tf_op jit(solution)/shard_map/psum | solution.py:188
  949.5 124.7 %psum.62 = f32[]{:T(128)} all-reduce(f32[]{:T(128)} %multiply_reduce_fusion.4), channel_id=1, replica_groups=mesh['grp'=12,'blk'=8,'sub'=8] {'blk','sub'}, use_global_device_ids=true, to_apply=%region_19.20 | all-reduce | flops 1 | bytes 8 | tf_op jit(solution)/shard_map/psum | solution.py:133
  1075.6 10.9 collective-permute-start.35
  1086.5 1.9 collective-permute-start.34
  1088.6 3.2 collective-permute-start.6
  1091.8 5.0 collective-permute-start.7
  1096.8 1.3 collective-permute-start.37
  1098.1 4.5 collective-permute-start.36
  1103.5 1.3 collective-permute-start.9
  1105.5 2.8 collective-permute-done.9
  1108.5 3.9 collective-permute-start.10
  1112.4 2.6 collective-permute-start.11
  1115.6 1.7 collective-permute-done.11
  1122.3 1.9 collective-permute-start.12
  1124.2 5.3 collective-permute-start.13
  1130.2 119.7 %psum.63 = f32[]{:T(128)} all-reduce(f32[]{:T(128)} %fusion.110), channel_id=1, replica_groups=mesh['grp'=12,'blk'=8,'sub'=8] {'blk','sub'}, use_global_device_ids=true, to_apply=%region_21.22 | all-reduce | flops 1 | bytes 8 | tf_op jit(solution)/shard_map/psum | solution.py:188
  1251.4 9.0 collective-permute-start.15
  1261.5 1.2 collective-permute-done.14
  1262.9 3.9 collective-permute-start.16
  1266.9 2.6 collective-permute-start.17
  1270.0 1.5 collective-permute-done.17
  (194 shorter events, 28.8 us)
Async XLA Ops:
  7.2 20.1 %copy-start.4 = (f32[8,8,128]{2,1,0:T(8,128)S(1)}, f32[8,8,128]{2,1,0:T(8,128)}, u32[]{:S(2)}) copy-start(f32[8,8,128]{2,1,0:T(8,128)} %param.61) | copy-start | bytes 98308
  7.2 265.2 %all-reduce.10.cloned.1.call-start = ((), (), s32[]{:S(2)}) async-start(), calls=%async_computation | async-start | bytes 524288
  8.2 69.5 %copy-start.27 = (s32[1,1,32]{2,1,0:T(1,128)S(1)}, s32[1,1,32]{2,1,0:T(1,128)}, u32[]{:S(2)}) copy-start(s32[1,1,32]{2,1,0:T(1,128)} %param.60) | copy-start | bytes 388
  9.1 69.3 %copy-start = (f32[4,32,128]{2,1,0:T(8,128)S(1)}, f32[4,32,128]{2,1,0:T(8,128)}, u32[]{:S(2)}) copy-start(f32[4,32,128]{2,1,0:T(8,128)} %param.57) | copy-start | bytes 196612
  9.1 69.3 %copy-start.15 = (f32[4,32,128]{2,1,0:T(8,128)S(1)}, f32[4,32,128]{2,1,0:T(8,128)}, u32[]{:S(2)}) copy-start(f32[4,32,128]{2,1,0:T(8,128)} %param.59) | copy-start | bytes 196612
  10.0 70.2 %copy-start.16 = (s32[8,8,128]{2,1,0:T(8,128)S(1)}, s32[8,8,128]{2,1,0:T(8,128)}, u32[]{:S(2)}) copy-start(s32[8,8,128]{2,1,0:T(8,128)} %param.63) | copy-start | bytes 98308
  10.0 70.2 %copy-start.28 = (f32[8]{0:T(128)S(1)}, f32[8]{0:T(128)}, u32[]{:S(2)}) copy-start(f32[8]{0:T(128)} %param.64) | copy-start | bytes 100
  10.2 78.0 %collective-permute-start.1 = (f32[5,4,32,1]{3,2,1,0:T(8,128)S(1)}, f32[5,4,32,1]{3,2,1,0:T(8,128)S(1)}, u32[]{:S(2)}, u32[]{:S(2)}) collective-permute-start(f32[5,4,32,1]{3,2,1,0:T(8,128)S(1)} %get-tuple-element.367), channel_id=1, source_target_pairs={{64,0},{128,64},{192,128},{256,192},{320,256},{384,320},{448,384},... | collective-permute-start | bytes 7688 | tf_op jit(solution)/shard_map/ppermute | solution.py:27
  25.3 62.9 %collective-permute-start = (f32[5,4,32,1]{3,2,1,0:T(8,128)S(1)}, f32[5,4,32,1]{3,2,1,0:T(8,128)S(1)}, u32[]{:S(2)}, u32[]{:S(2)}) collective-permute-start(f32[5,4,32,1]{3,2,1,0:T(8,128)S(1)} %get-tuple-element.368), channel_id=1, source_target_pairs={{0,64},{64,128},{128,192},{192,256},{256,320},{320,384},{384,448},... | collective-permute-start | bytes 7688 | tf_op jit(solution)/shard_map/ppermute | solution.py:24
  27.3 55.0 %collective-permute-start.18 = (f32[1,8,128]{2,1,0:T(8,128)S(1)}, f32[1,8,128]{2,1,0:T(8,128)S(1)}, u32[]{:S(2)}, u32[]{:S(2)}) collective-permute-start(f32[1,8,128]{2,1,0:T(8,128)S(1)} %get-tuple-element.397), channel_id=1, source_target_pairs={{0,8},{8,16},{16,24},{24,32},{32,40},{40,48},{48,56},{1,9},{9,17},... | collective-permute-start | bytes 12296 | tf_op jit(solution)/shard_map/ppermute | solution.py:24
  31.2 51.6 %collective-permute-start.19 = (f32[1,8,128]{2,1,0:T(8,128)S(1)}, f32[1,8,128]{2,1,0:T(8,128)S(1)}, u32[]{:S(2)}, u32[]{:S(2)}) collective-permute-start(f32[1,8,128]{2,1,0:T(8,128)S(1)} %get-tuple-element.398), channel_id=1, source_target_pairs={{8,0},{16,8},{24,16},{32,24},{40,32},{48,40},{56,48},{9,1},{17,9},... | collective-permute-start | bytes 12296 | tf_op jit(solution)/shard_map/ppermute | solution.py:27
  82.8 10.5 copy-start.5
  82.9 10.5 copy-start.23
  82.9 10.5 copy-start.12
  82.9 7.9 collective-permute-start.21
  84.2 6.6 collective-permute-start.20
  88.4 4.8 collective-permute-start.3
  89.9 3.3 collective-permute-start.2
  90.8 9.7 copy-start.17
  90.8 9.7 copy-start.19
  93.4 7.1 collective-permute-start.5
  95.3 5.8 collective-permute-start.4
  100.5 2.2 copy-start.7
  104.9 167.5 %copy-start.14 = (f32[8,8,128]{2,1,0:T(8,128)S(1)}, f32[8,8,128]{2,1,0:T(8,128)}, u32[]{:S(2)}) copy-start(f32[8,8,128]{2,1,0:T(8,128)} %copy.36) | copy-start | bytes 98308
  104.9 168.1 %copy-start.2 = (f32[6,8,8,128]{3,2,1,0:T(8,128)S(1)}, f32[6,8,8,128]{3,2,1,0:T(8,128)}, u32[]{:S(2)}) copy-start(f32[6,8,8,128]{3,2,1,0:T(8,128)} %param.62) | copy-start | bytes 589828
  104.9 168.1 %copy-start.6 = (f32[8,8,128]{2,1,0:T(8,128)S(1)}, f32[8,8,128]{2,1,0:T(8,128)}, u32[]{:S(2)}) copy-start(f32[8,8,128]{2,1,0:T(8,128)} %copy-done.5) | copy-start | bytes 98308
  104.9 168.1 %copy-start.13 = (f32[10,8,128]{2,1,0:T(8,128)S(1)}, f32[10,8,128]{2,1,0:T(8,128)}, u32[]{:S(2)}) copy-start(f32[10,8,128]{2,1,0:T(8,128)} %copy-done.12) | copy-start | bytes 122884
  104.9 168.1 %copy-start.18 = (f32[10,1,128]{2,1,0:T(1,128)S(1)}, f32[10,1,128]{2,1,0:T(1,128)}, u32[]{:S(2)}) copy-start(f32[10,1,128]{2,1,0:T(1,128)} %copy-done.17) | copy-start | bytes 15364
  105.0 168.1 %copy-start.20 = (f32[10,1,128]{2,1,0:T(1,128)S(1)}, f32[10,1,128]{2,1,0:T(1,128)}, u32[]{:S(2)}) copy-start(f32[10,1,128]{2,1,0:T(1,128)} %copy-done.19) | copy-start | bytes 15364
  105.0 168.1 %copy-start.22 = (f32[1,8,128]{2,1,0:T(8,128)S(1)}, f32[1,8,128]{2,1,0:T(8,128)}, u32[]{:S(2)}) copy-start(f32[1,8,128]{2,1,0:T(8,128)} %copy-done.21) | copy-start | bytes 12292
  105.0 168.1 %copy-start.24 = (f32[1,8,128]{2,1,0:T(8,128)S(1)}, f32[1,8,128]{2,1,0:T(8,128)}, u32[]{:S(2)}) copy-start(f32[1,8,128]{2,1,0:T(8,128)} %copy-done.23) | copy-start | bytes 12292
  105.0 180.9 %copy-start.8 = (f32[5,6,1,130]{3,2,1,0:T(1,128)S(1)}, f32[5,6,1,130]{3,2,1,0:T(1,128)}, u32[]{:S(2)}) copy-start(f32[5,6,1,130]{3,2,1,0:T(1,128)} %copy-done.7) | copy-start | bytes 46804
  105.0 180.9 %copy-start.10 = (f32[5,6,1,130]{3,2,1,0:T(1,128)S(1)}, f32[5,6,1,130]{3,2,1,0:T(1,128)}, u32[]{:S(2)}) copy-start(f32[5,6,1,130]{3,2,1,0:T(1,128)} %copy-done.9) | copy-start | bytes 46804
  274.2 6.3 collective-permute-start.23
  276.1 4.4 collective-permute-start.22
  280.6 7.4 collective-permute-start.25
  281.9 6.1 collective-permute-start.24
  288.8 260.3 %copy-start.3 = (f32[6,34,130]{2,1,0:T(8,128)S(1)}, f32[6,34,130]{2,1,0:T(8,128)}, u32[]{:S(2)}) copy-start(f32[6,34,130]{2,1,0:T(8,128)} %get-tuple-element.301) | copy-start | bytes 318244
  536.3 13.0 %collective-permute-start.27 = (f32[1,8,128]{2,1,0:T(8,128)S(1)}, f32[1,8,128]{2,1,0:T(8,128)S(1)}, u32[]{:S(2)}, u32[]{:S(2)}) collective-permute-start(f32[1,8,128]{2,1,0:T(8,128)S(1)} %get-tuple-element.392), channel_id=1, source_target_pairs={{8,0},{16,8},{24,16},{32,24},{40,32},{48,40},{56,48},{9,1},{17,9},... | collective-permute-start | bytes 12296 | tf_op jit(solution)/shard_map/ppermute | solution.py:27
  547.2 3.1 collective-permute-start.26
  550.3 7.8 collective-permute-start.29
  551.6 6.5 collective-permute-start.28
  555.6 262.9 %copy-start.25 = (f32[5]{0:T(128)S(1)}, f32[5]{0:T(128)}, u32[]{:S(2)}) copy-start(f32[5]{0:T(128)} %constant.577) | copy-start | bytes 64
  805.7 15.4 %collective-permute-start.31 = (f32[1,8,128]{2,1,0:T(8,128)S(1)}, f32[1,8,128]{2,1,0:T(8,128)S(1)}, u32[]{:S(2)}, u32[]{:S(2)}) collective-permute-start(f32[1,8,128]{2,1,0:T(8,128)S(1)} %get-tuple-element.390), channel_id=1, source_target_pairs={{8,0},{16,8},{24,16},{32,24},{40,32},{48,40},{56,48},{9,1},{17,9},... | collective-permute-start | bytes 12296 | tf_op jit(solution)/shard_map/ppermute | solution.py:27
  816.6 4.5 collective-permute-start.30
  818.5 7.9 copy-start.11
  821.1 5.3 collective-permute-start.33
  822.4 4.7 collective-permute-start.32
  1075.6 21.2 %collective-permute-start.35 = (f32[1,8,128]{2,1,0:T(8,128)S(1)}, f32[1,8,128]{2,1,0:T(8,128)S(1)}, u32[]{:S(2)}, u32[]{:S(2)}) collective-permute-start(f32[1,8,128]{2,1,0:T(8,128)S(1)} %get-tuple-element.388), channel_id=1, source_target_pairs={{8,0},{16,8},{24,16},{32,24},{40,32},{48,40},{56,48},{9,1},{17,9},... | collective-permute-start | bytes 12296 | tf_op jit(solution)/shard_map/ppermute | solution.py:27
  1086.5 10.3 collective-permute-start.34
  1088.6 14.0 %collective-permute-start.6 = (f32[5,4,32,1]{3,2,1,0:T(8,128)S(1)}, f32[5,4,32,1]{3,2,1,0:T(8,128)S(1)}, u32[]{:S(2)}, u32[]{:S(2)}) collective-permute-start(f32[5,4,32,1]{3,2,1,0:T(8,128)S(1)} %get-tuple-element.366), channel_id=1, source_target_pairs={{0,64},{64,128},{128,192},{192,256},{256,320},{320,384},{384,448},... | collective-permute-start | bytes 7688 | tf_op jit(solution)/shard_map/ppermute | solution.py:24
  1091.8 11.5 collective-permute-start.7
  1096.8 8.5 collective-permute-start.37
  1098.1 7.2 collective-permute-start.36
  1103.5 4.8 collective-permute-start.9
  1104.9 3.4 collective-permute-start.8
  1108.5 7.1 collective-permute-start.10
  1112.4 4.9 collective-permute-start.11
  1122.3 129.0 %collective-permute-start.12 = (f32[5,4,32,1]{3,2,1,0:T(8,128)S(1)}, f32[5,4,32,1]{3,2,1,0:T(8,128)S(1)}, u32[]{:S(2)}, u32[]{:S(2)}) collective-permute-start(f32[5,4,32,1]{3,2,1,0:T(8,128)S(1)} %get-tuple-element.364), channel_id=1, source_target_pairs={{0,64},{64,128},{128,192},{192,256},{256,320},{320,384},{384,448},... | collective-permute-start | bytes 7688 | tf_op jit(solution)/shard_map/ppermute | solution.py:24
  1124.2 127.0 %collective-permute-start.13 = (f32[5,4,32,1]{3,2,1,0:T(8,128)S(1)}, f32[5,4,32,1]{3,2,1,0:T(8,128)S(1)}, u32[]{:S(2)}, u32[]{:S(2)}) collective-permute-start(f32[5,4,32,1]{3,2,1,0:T(8,128)S(1)} %get-tuple-element.363), channel_id=1, source_target_pairs={{64,0},{128,64},{192,128},{256,192},{320,256},{384,320},{448,384},... | collective-permute-start | bytes 7688 | tf_op jit(solution)/shard_map/ppermute | solution.py:27
  1251.4 10.1 collective-permute-start.15
  1260.5 2.3 collective-permute-start.14
  1262.9 7.1 collective-permute-start.16
  1266.9 4.6 collective-permute-start.17
  (4 other events, 3.8 us)
Sparse Core Ops, SparseCore 0:
  79.6 192.7 all-reduce.9
where the time goes:
time: 1290 us; the launch traced here: 1280 us
  blocking collectives  894 us (69%)
  waiting for transfers between devices  178 us (14%)
  starting transfers between devices  140 us (11%)
  other arithmetic  39.8 us (3%)
  between operations  25.4 us (2%)
    psum x4, blocking collectives, squared_sum(): return lax.psum(jnp.sum(equation_misfit * equation_misfit), ('blk', 'sub'))  492 us
    psum x3, blocking collectives, shards(): lax.psum(jnp.sum(search_vector * image_dir), ('blk', 'sub'))  357 us
    unnamed x2, waiting for transfers between devices  166 us
    ppermute x19, starting transfers between devices, extended(): lax.ppermute(lax.slice_in_dim(block, 0, width, axis=dim), axis, backward)  87.4 us
    ppermute x19, starting transfers between devices, extended(): lax.ppermute(lax.slice_in_dim(block, block.shape[dim] - width, None, axis...  52.7 us
    all_gather x1, blocking collectives, shards(): lax.all_gather(surface_kelvin, ('blk', 'sub'), axis=0, tiled=True)  44.5 us
  transfers between devices with their start and end apart: 39, of which 11 were waited for; matrix products, arithmetic and copies ran while one was open for 2% of the time, Pallas kernels for 0%

commit v1 on v0

v1 whole, which is shorter than its diff:
```python
import jax
import jax.numpy as jnp
from jax import lax
from jax.experimental import pallas as pl
from jax.experimental.pallas import tpu as pltpu
from jax.sharding import PartitionSpec as P

ITERS = 4
DT = 0.1
NU = 0.05
GM1 = 0.4
GAMMA = 1.4
SHIFT = 8.0
WIDTH = 8.0
ID = pl.DeviceIdType.MESH
F32 = jnp.float32


def primitives(u):
    inv = 1.0 / u[0]
    vel = [u[1] * inv, u[2] * inv, u[3] * inv]
    kin = 0.5 * (u[1] * vel[0] + u[2] * vel[1] + u[3] * vel[2])
    p = GM1 * (u[4] - kin)
    c = jnp.sqrt(GAMMA * p * inv)
    return vel[0], vel[1], vel[2], p, c


def flux(u, vel, p, d):
    out = [u[1 + d], u[1] * vel, u[2] * vel, u[3] * vel, (u[4] + p) * vel]
    out[1 + d] = out[1 + d] + p
    return out


def face(lo, hi):
    s = jnp.maximum(lo[2], hi[2])
    sv = s + 2.0 * NU
    return [
        (lo[1][f] + hi[1][f]) - (s if f == 0 else sv) * (hi[0][f] - lo[0][f])
        for f in range(5)
    ]


def kernel(
    rho_ref, vel_ref, p_ref, idx_ref, x0_ref, fc_ref, mat_ref, cap_ref,
    fluid_ref, metal_ref,
    us, pr, hz, yp, yr, zp, zr, sink, ft,
    rb1, rw, hc, rhc, wb, rwb,
    fm, pk_lo, pk_hi, rl, rh, wm, fr, qk_lo, qk_hi, ql, qh, vk, mom, rmom,
    b1_s, b1_r, y1_s, y1_r, y2_s, y2_r, b2_s, b2_r, fs, frv, ms, mr, rs, rr_, as_, ar,
):
    me_g = lax.axis_index("grp")
    me_b = lax.axis_index("blk")
    me_s = lax.axis_index("sub")
    ng = lax.axis_size("grp")
    nb = lax.axis_size("blk")
    nsub = lax.axis_size("sub")

    def blk(k):
        return lax.rem(me_b + (k + nb), nb)

    def sub(k):
        return lax.rem(me_s + (k + nsub), nsub)

    def grp(k):
        return lax.rem(me_g + (k + ng), ng)

    zlo, zhi = {"grp": grp(-1)}, {"grp": grp(1)}
    partners = [{"blk": blk(k)} for k in range(1, nb)]
    partners += [{"sub": sub(k)} for k in range(1, nsub)]
    partners += [zlo, zhi]
    partners += [{"blk": blk(i), "sub": sub(j)} for i in (-1, 1) for j in (-1, 1)]
    barrier = pltpu.get_barrier_semaphore()
    for d in partners:
        pl.semaphore_signal(barrier, inc=1, device_id=d, device_id_type=ID)

    def rcopy(src, dst, s, r, dev):
        return pltpu.make_async_remote_copy(
            src_ref=src, dst_ref=dst, send_sem=s, recv_sem=r, device_id=dev, device_id_type=ID
        )

    lane8 = lax.broadcasted_iota(jnp.int32, (8, 128), 1)
    sub8 = lax.broadcasted_iota(jnp.int32, (8, 128), 0)
    low4 = sub8 < 4

    def start_x(x, _):
        rho = rho_ref[x]
        v = [vel_ref[k, x] for k in range(3)]
        mo = [rho * a for a in v]
        us[0, 0, 1 + x, 8:40, :] = rho
        for k in range(3):
            us[0, 1 + k, 1 + x, 8:40, :] = mo[k]
        us[0, 4, 1 + x, 8:40, :] = p_ref[x] / GM1 + 0.5 * (
            mo[0] * v[0] + mo[1] * v[1] + mo[2] * v[2]
        )
        return 0

    lax.fori_loop(0, 4, start_x, 0)

    def pack_fluid(st):
        lane = lax.broadcasted_iota(jnp.int32, (32, 128), 1)
        acc = jnp.zeros((32, 128), F32)
        for x in range(4):
            for f in range(5):
                j = x * 5 + f
                yp[st, 0, j : j + 1, :] = us[st, f, 1 + x, 8:9, :]
                yp[st, 1, j : j + 1, :] = us[st, f, 1 + x, 39:40, :]
                tile = pltpu.roll(us[st, f, 1 + x, 8:40, :], 2 * j + 1, 1)
                acc = jnp.where((lane == 2 * j) | (lane == 2 * j + 1), tile, acc)
        zp[st] = acc

    def fluid_copies(st):
        rows = pl.ds(8, 32)
        return [
            rcopy(us.at[st, :, 1, rows, :], us.at[st, :, 5, rows, :], fs.at[st, 0], frv.at[st, 0], {"blk": blk(-1)}),
            rcopy(us.at[st, :, 4, rows, :], us.at[st, :, 0, rows, :], fs.at[st, 1], frv.at[st, 1], {"blk": blk(1)}),
            rcopy(yp.at[st, 0], yr.at[st, 1], fs.at[st, 2], frv.at[st, 2], {"sub": sub(-1)}),
            rcopy(yp.at[st, 1], yr.at[st, 0], fs.at[st, 3], frv.at[st, 3], {"sub": sub(1)}),
            rcopy(zp.at[st], zr.at[st, 0], fs.at[st, 4], frv.at[st, 4], zhi),
            rcopy(zp.at[st], zr.at[st, 1], fs.at[st, 5], frv.at[st, 5], zlo),
        ]

    pack_fluid(0)

    idx = idx_ref[0]
    dev_of = lax.shift_right_logical(idx, 3)
    slot1 = ((idx & 7) + 1).astype(F32)
    hot = lax.broadcasted_iota(jnp.int32, (64, 32), 0) == jnp.broadcast_to(dev_of, (64, 32))
    face_temp = p_ref[0] / rho_ref[0]
    by_dev = jnp.dot(
        hot.astype(F32), face_temp, precision=lax.Precision.HIGHEST, preferred_element_type=F32
    )
    slot_of = jnp.sum(jnp.where(hot, jnp.broadcast_to(slot1, (64, 32)), 0.0), axis=1, keepdims=True)
    slot_rows = jnp.broadcast_to(slot_of, (64, 128))
    for m in range(8):
        ft[m, 0] = by_dev[8 * m : 8 * m + 8]
        ft[m, 1] = slot_rows[8 * m : 8 * m + 8]

    for x in range(8):
        mat = mat_ref[x]
        cap = jnp.zeros((8, 128), F32)
        for m in range(8):
            cap = jnp.where(mat == m, cap_ref[m], cap)
        k = [fc_ref[f, x] for f in range(6)]
        diag = cap + ((k[0] + k[3]) + (k[1] + k[4]) + (k[2] + k[5]))
        fm[0, 4 + x] = x0_ref[x]
        fm[1, 4 + x] = (diag - SHIFT) * (1.0 / WIDTH)
        for f in range(3):
            fm[2 + f, 4 + x] = k[f] * (1.0 / WIDTH)

    def pack_metal(field, lo, hi):
        for t in range(4):
            a, b = field(2 * t), field(2 * t + 1)
            lo[t] = jnp.where(low4, a, pltpu.roll(b, 4, 0))
            hi[t] = jnp.where(low4, pltpu.roll(a, 4, 0), b)

    for f in range(5):
        pack_metal(lambda x: fm[f, 4 + x], pk_lo.at[f], pk_hi.at[f])

    def metal_copies(body, lo, hi, dl, dh, s, r):
        def cut(ref, a, b):
            return ref.at[:, a:b]

        return [
            rcopy(cut(body, 8, 12), cut(body, 0, 4), s.at[0], r.at[0], {"blk": blk(1)}),
            rcopy(cut(body, 4, 8), cut(body, 12, 16), s.at[1], r.at[1], {"blk": blk(-1)}),
            rcopy(hi, cut(dl, 2, 6), s.at[2], r.at[2], {"sub": sub(1)}),
            rcopy(lo, cut(dh, 2, 6), s.at[3], r.at[3], {"sub": sub(-1)}),
            rcopy(cut(hi, 2, 4), cut(dl, 0, 2), s.at[4], r.at[4], {"blk": blk(1), "sub": sub(1)}),
            rcopy(cut(hi, 0, 2), cut(dl, 6, 8), s.at[5], r.at[5], {"blk": blk(-1), "sub": sub(1)}),
            rcopy(cut(lo, 2, 4), cut(dh, 0, 2), s.at[6], r.at[6], {"blk": blk(1), "sub": sub(-1)}),
            rcopy(cut(lo, 0, 2), cut(dh, 6, 8), s.at[7], r.at[7], {"blk": blk(-1), "sub": sub(-1)}),
        ]

    rb1[me_b] = ft[me_b]
    rw[me_s] = x0_ref[0]

    pl.semaphore_wait(barrier, len(partners))

    for k in range(1, nb):
        to = blk(k)
        rcopy(ft.at[to], rb1.at[me_b], b1_s, b1_r, {"blk": to}).start()
    for k in range(1, nsub):
        rcopy(x0_ref.at[0], rw.at[me_s], y1_s, y1_r, {"sub": sub(k)}).start()
    halo = [fluid_copies(st) for st in range(3)]
    for c in halo[0]:
        c.start()
    coarse = metal_copies(fm, pk_lo, pk_hi, rl, rh, ms, mr)
    for c in coarse:
        c.start()

    def prims_at(st, x, r0, n):
        u = [us[st, f, x, r0 : r0 + n, :] for f in range(5)]
        for k, val in enumerate(primitives(u)):
            pr[k, x, r0 : r0 + n, :] = val

    def own_prims(st):
        def body(x, _):
            prims_at(st, x, 8, 32)
            return 0

        lax.fori_loop(1, 5, body, 0)

    def halo_in(st):
        for c in halo[st]:
            c.wait_recv()
        for x in range(4):
            for f in range(5):
                j = x * 5 + f
                us[st, f, 1 + x, 7:8, :] = yr[st, 0, j : j + 1, :]
                us[st, f, 1 + x, 40:41, :] = yr[st, 1, j : j + 1, :]
        prims_at(st, 0, 8, 32)
        prims_at(st, 5, 8, 32)
        lane = lax.broadcasted_iota(jnp.int32, (32, 128), 1)
        both = jnp.where((lane & 1) == 0, zr[st, 0], pltpu.roll(zr[st, 1], 126, 1))

        def body(x, _):
            prims_at(st, 1 + x, 0, 8)
            prims_at(st, 1 + x, 40, 8)
            u = [pltpu.roll(both, 128 - 2 * (x * 5 + f), 1) for f in range(5)]
            q = primitives(u)
            for f in range(5):
                hz[f, x] = u[f]
            for f, val in enumerate((q[2], q[3], q[4])):
                hz[5 + f, x] = val
            return 0

        lax.fori_loop(0, 4, body, 0)

    def stage(st, with_sink):
        first, last = lane8 == 0, lane8 == 127

        def body(x, _):
            for t in range(4):
                r = 8 + 8 * t

                def cells(dx, dr, d):
                    u = [us[st, f, 1 + x + dx, r + dr : r + dr + 8, :] for f in range(5)]
                    v = pr[d, 1 + x + dx, r + dr : r + dr + 8, :]
                    p = pr[3, 1 + x + dx, r + dr : r + dr + 8, :]
                    c = pr[4, 1 + x + dx, r + dr : r + dr + 8, :]
                    return u, flux(u, v, p, d), jnp.abs(v) + c

                mid = [cells(0, 0, d) for d in range(3)]
                u = mid[0][0]
                rate = None
                for d, lo, hi in (
                    (0, cells(-1, 0, 0), cells(1, 0, 0)),
                    (1, cells(0, -1, 1), cells(0, 1, 1)),
                ):
                    g0, g1 = face(lo, mid[d]), face(mid[d], hi)
                    part = [a - b for a, b in zip(g0, g1)]
                    rate = part if rate is None else [a + b for a, b in zip(rate, part)]
                h = [hz[f, x, r - 8 : r, :] for f in range(8)]
                q = list(u) + [pr[k, 1 + x, r : r + 8, :] for k in (2, 3, 4)]
                for shift, edge, low in ((1, first, True), (127, last, False)):
                    n = [jnp.where(edge, a, pltpu.roll(b, shift, 1)) for a, b in zip(h, q)]
                    other = (n[:5], flux(n[:5], n[5], n[6], 2), jnp.abs(n[5]) + n[7])
                    if low:
                        rate = [a + b for a, b in zip(rate, face(other, mid[2]))]
                    else:
                        rate = [a - b for a, b in zip(rate, face(mid[2], other))]
                for f in range(5):
                    new = u[f] + (0.5 * DT) * rate[f]
                    if with_sink and f == 4:
                        new = new - DT * sink[x, r - 8 : r, :]
                    if st == 1:
                        new = 0.75 * us[0, f, 1 + x, r : r + 8, :] + 0.25 * new
                    if st == 2:
                        new = (1.0 / 3.0) * us[0, f, 1 + x, r : r + 8, :] + (2.0 / 3.0) * new
                        fluid_ref[f, x, r - 8 : r, :] = new
                    else:
                        us[st + 1, f, 1 + x, r : r + 8, :] = new
            return 0

        lax.fori_loop(0, 4, body, 0)

    own_prims(0)

    def wait_all(buf, s, r, dev):
        d = rcopy(buf, buf, s, r, dev)
        return d

    near_b, near_s = {"blk": blk(1)}, {"sub": sub(1)}

    wait_all(rb1.at[0:7], b1_s, b1_r, near_b).wait_recv()

    def gather_strips(m, _):
        total = jnp.zeros((8, 128), F32)
        count = jnp.zeros((8, 128), F32)
        want = (sub8 + 1).astype(F32)
        for b in range(8):
            val = jnp.broadcast_to(rb1[b, 0, pl.ds(m, 1), :], (8, 128))
            slot = jnp.broadcast_to(rb1[b, 1, pl.ds(m, 1), :], (8, 128))
            here = slot == want
            total = total + jnp.where(here, val, 0.0)
            count = count + jnp.where(here, 1.0, 0.0)
        hc[m, 0] = total
        hc[m, 1] = count
        return 0

    lax.fori_loop(0, 8, gather_strips, 0)
    rhc[me_s] = hc[me_s]
    for k in range(1, nsub):
        to = sub(k)
        rcopy(hc.at[to], rhc.at[me_s], y2_s, y2_r, {"sub": to}).start()

    wait_all(rw.at[0:7], y1_s, y1_r, near_s).wait_recv()
    walls = jnp.concatenate([rw[m] for m in range(8)], axis=0)
    slots = jnp.concatenate([rb1[b, 1] for b in range(8)], axis=0)[:, 0:64]
    row = lax.broadcasted_iota(jnp.int32, (64, 64), 0)
    col = lax.broadcasted_iota(jnp.int32, (64, 64), 1)
    pick = (lax.shift_right_logical(col, 3) == (row & 7)) & (((col & 7) + 1).astype(F32) == slots)
    wall_rows = jnp.dot(
        pick.astype(F32), walls, precision=lax.Precision.HIGHEST, preferred_element_type=F32
    )
    for b in range(8):
        wb[b] = wall_rows[8 * b : 8 * b + 8]
    rwb[me_b] = wb[me_b]
    for k in range(1, nb):
        to = blk(k)
        rcopy(wb.at[to], rwb.at[me_b], b2_s, b2_r, {"blk": to}).start()

    halo_in(0)
    stage(0, False)

    wait_all(rwb.at[0:7], b2_s, b2_r, near_b).wait_recv()
    lane32 = lax.broadcasted_iota(jnp.int32, (32, 128), 1)
    sub32 = lax.broadcasted_iota(jnp.int32, (32, 32), 0)
    eye = sub32 == lax.broadcasted_iota(jnp.int32, (32, 32), 1)
    dev_f = jnp.broadcast_to(dev_of.astype(F32), (32, 32))
    dev_col = jnp.sum(jnp.where(eye, dev_f, 0.0), axis=1, keepdims=True)
    hot_t = lax.broadcasted_iota(jnp.int32, (32, 64), 1).astype(F32) == jnp.broadcast_to(dev_col, (32, 64))
    seen = jnp.concatenate([rwb[b] for b in range(8)], axis=0)
    wall_seen = jnp.dot(
        hot_t.astype(F32), seen, precision=lax.Precision.HIGHEST, preferred_element_type=F32
    )
    heat_flux = p_ref[0] / rho_ref[0] - wall_seen
    sink[0] = heat_flux
    for x in range(1, 4):
        sink[x] = jnp.zeros((32, 128), F32)
    us[1, 4, 1, 8:40, :] = us[1, 4, 1, 8:40, :] - DT * heat_flux
    pack_fluid(1)
    for c in halo[1]:
        c.start()

    for c in coarse:
        c.wait_recv()

    def window(x, mid, lo, hi, odd):
        turned = pltpu.roll(mid, 4, 0)
        if odd:
            lo = pltpu.roll(lo, 4, 0)
        else:
            hi = pltpu.roll(hi, 4, 0)
        return jnp.where(low4, lo, turned), jnp.where(low4, turned, hi)

    def build(f, _):
        for x in range(16):
            w0, w1 = window(x, fm[f, x], rl[f, x // 2], rh[f, x // 2], x % 2)
            wm[f, x, 0:8, :] = w0
            wm[f, x, 8:16, :] = w1
        return 0

    lax.fori_loop(0, 5, build, 0)

    def laplace(x):
        v = wm[0, x]
        ky, kz = wm[3, x], wm[4, x]
        gy = ky * (v - pltpu.roll(v, 1, 0))
        gz = kz * (v - pltpu.roll(v, 1, 1))
        out = wm[2, x] * (v - wm[0, x - 1]) + wm[2, x + 1] * (v - wm[0, x + 1])
        return out + (gy - pltpu.roll(gy, 15, 0)) + (gz - pltpu.roll(gz, 127, 1))

    wait_all(rhc.at[0:7], y2_s, y2_r, near_s).wait_recv()
    total = rhc[0, 0]
    count = rhc[0, 1]
    for m in range(1, 8):
        total = total + rhc[m, 0]
        count = count + rhc[m, 1]
    heat_in = total - count * x0_ref[0]

    def start_r(x, _):
        lap = laplace(4 + x)
        fr[0, 4 + x] = pltpu.roll(jnp.where(low4, lap[8:16], lap[0:8]), 4, 0) * (-WIDTH)
        return 0

    lax.fori_loop(0, 8, start_r, 0)
    fr[0, 4] = fr[0, 4] + heat_in
    pack_metal(lambda x: fr[0, 4 + x], qk_lo.at[0], qk_hi.at[0])
    fine = metal_copies(fr, qk_lo, qk_hi, ql, qh, rs, rr_)
    for c in fine:
        c.start()

    own_prims(1)
    halo_in(1)
    stage(1, True)
    pack_fluid(2)
    for c in halo[2]:
        c.start()

    for c in fine:
        c.wait_recv()
    for x in range(16):
        w0, w1 = window(x, fr[0, x], ql[0, x // 2], qh[0, x // 2], x % 2)
        vk[0, x, 0:8, :] = w0
        vk[0, x, 8:16, :] = w1

    for n in range(4):

        def apply(x, _):
            v = vk[n, x]
            ky, kz = wm[3, x], wm[4, x]
            out = wm[1, x] * v - wm[2, x] * vk[n, x - 1] - wm[2, x + 1] * vk[n, x + 1]
            out = out - ky * pltpu.roll(v, 1, 0) - pltpu.roll(ky, 15, 0) * pltpu.roll(v, 15, 0)
            out = out - kz * pltpu.roll(v, 1, 1) - pltpu.roll(kz, 127, 1) * pltpu.roll(v, 127, 1)
            vk[n + 1, x] = out
            return 0

        lax.fori_loop(n + 1, 15 - n, apply, 0)

    def dots(x, acc):
        v = [vk[n, x, 4:12, :] for n in range(5)]
        return tuple(a + v[k // 2] * v[(k + 1) // 2] for k, a in enumerate(acc))

    acc = lax.fori_loop(4, 12, dots, tuple(jnp.zeros((8, 128), F32) for _ in range(8)))
    tile = jnp.zeros((8, 128), F32)
    for k in range(8):
        tile = jnp.where(sub8 == k, jnp.sum(acc[k], axis=0, keepdims=True), tile)
    col8 = jnp.sum(tile, axis=1, keepdims=True)
    mom[...] = jnp.sum(jnp.where(lane8 == sub8, col8, 0.0), axis=0, keepdims=True)
    mine = me_b * 8 + me_s
    rmom[mine] = mom[...]

    def send_moments(k, _):
        to = {
            "blk": lax.rem(me_b + k // 8, 8),
            "sub": lax.rem(me_s + k % 8, 8),
        }
        rcopy(mom, rmom.at[mine], as_, ar, to).start()
        return 0

    lax.fori_loop(1, 64, send_moments, 0)

    own_prims(2)
    halo_in(2)
    stage(2, True)

    wait_all(rmom.at[0:63], as_, ar, near_b).wait_recv()
    sums = jnp.sum(rmom[...], axis=0)
    lane1 = lax.broadcasted_iota(jnp.int32, (1, 128), 1)
    m = [jnp.sum(jnp.where(lane1 == k, sums, 0.0), axis=1, keepdims=True) for k in range(8)]

    def product(p, q):
        out = None
        for i, a in enumerate(p):
            inner = None
            for j, b in enumerate(q):
                inner = m[i + j] * b if inner is None else inner + m[i + j] * b
            out = a * inner if out is None else out + a * inner
        return out

    def times_a(p):
        out = [SHIFT * a for a in p] + [jnp.zeros_like(p[0])]
        for i, a in enumerate(p):
            out[i + 1] = out[i + 1] + WIDTH * a
        return out

    def ratio(a, b):
        ok = b > 0.0
        return jnp.where(ok, a / jnp.where(ok, b, 1.0), 0.0)

    one = jnp.ones((1, 1), F32)
    r, d = [one], [one]
    coef = [jnp.zeros((1, 1), F32) for _ in range(4)]
    norm = m[0]
    for step in range(ITERS):
        image = times_a(d)
        alpha = ratio(norm, product(d, image))
        for i, a in enumerate(d):
            coef[i] = coef[i] + alpha * a
        if step == ITERS - 1:
            break
        r = [
            (r[i] if i < len(r) else 0.0) - alpha * image[i] for i in range(len(image))
        ]
        new = jnp.maximum(product(r, r), 0.0)
        beta = ratio(new, norm)
        d = [r[i] + (beta * d[i] if i < len(d) else 0.0) for i in range(len(r))]
        norm = new

    for x in range(8):
        out = x0_ref[x]
        for n in range(4):
            out = out + coef[n] * vk[n, 4 + x, 4:12, :]
        metal_ref[x] = out

    wait_all(rb1.at[0:7], b1_s, b1_r, near_b).wait_send()
    wait_all(rw.at[0:7], y1_s, y1_r, near_s).wait_send()
    wait_all(rhc.at[0:7], y2_s, y2_r, near_s).wait_send()
    wait_all(rwb.at[0:7], b2_s, b2_r, near_b).wait_send()
    for c in halo[0] + halo[1] + halo[2] + coarse + fine:
        c.wait_send()
    wait_all(rmom.at[0:63], as_, ar, near_b).wait_send()


def shards(rho, vel, p, idx, x0, fc, mat, cap):
    vmem = pl.BlockSpec(memory_space=pltpu.VMEM)
    dma = pltpu.SemaphoreType.DMA

    def buf(*shape):
        return pltpu.VMEM(shape, F32)

    return pl.pallas_call(
        kernel,
        out_shape=(
            jax.ShapeDtypeStruct((5, 4, 32, 128), F32),
            jax.ShapeDtypeStruct((8, 8, 128), F32),
        ),
        in_specs=[vmem] * 7 + [pl.BlockSpec(memory_space=pltpu.SMEM)],
        out_specs=(vmem, vmem),
        scratch_shapes=[
            buf(3, 5, 6, 48, 128), buf(5, 6, 48, 128), buf(8, 4, 32, 128),
            buf(3, 2, 24, 128), buf(3, 2, 24, 128), buf(3, 32, 128), buf(3, 2, 32, 128),
            buf(4, 32, 128), buf(8, 2, 8, 128),
            buf(8, 2, 8, 128), buf(8, 8, 128), buf(8, 2, 8, 128), buf(8, 2, 8, 128),
            buf(8, 8, 128), buf(8, 8, 128),
            buf(5, 16, 8, 128), buf(5, 4, 8, 128), buf(5, 4, 8, 128),
            buf(5, 8, 8, 128), buf(5, 8, 8, 128), buf(5, 16, 16, 128),
            buf(1, 16, 8, 128), buf(1, 4, 8, 128), buf(1, 4, 8, 128),
            buf(1, 8, 8, 128), buf(1, 8, 8, 128), buf(5, 16, 16, 128),
            buf(1, 128), buf(64, 1, 128),
            dma, dma, dma, dma, dma, dma, dma, dma,
            dma((3, 6)), dma((3, 6)), dma((8,)), dma((8,)), dma((8,)), dma((8,)), dma, dma,
        ],
        compiler_params=pltpu.CompilerParams(
            collective_id=0, has_side_effects=True, vmem_limit_bytes=32 * 1024 * 1024
        ),
    )(rho, vel, p, idx, x0, fc, mat, cap)


def solution(mesh):
    in_specs = (
        P("blk", "sub", "grp"),
        P(None, "blk", "sub", "grp"),
        P("blk", "sub", "grp"),
        P("grp", "blk", "sub"),
        P("blk", "sub", "grp"),
        P(None, "blk", "sub", "grp"),
        P("blk", "sub", "grp"),
        P(),
    )
    out_specs = (P(None, "blk", "sub", "grp"), P("blk", "sub", "grp"))
    return jax.shard_map(shards, mesh=mesh, in_specs=in_specs, out_specs=out_specs, check_vma=False)
```

time: 1290 us -> 53.5 us (0.04)
  blocking collectives: 894 us -> 0 us
  waiting for transfers between devices: 178 us -> 0 us
  starting transfers between devices: 140 us -> 0 us
  Pallas kernels: 0 us -> 44.8 us
  other arithmetic: 39.8 us -> 0 us
  between operations: 25.4 us -> 0.66 us
    psum x7 -> x0, blocking collectives: 850 us -> none  [the longest x4 492 us: squared_sum(): return lax.psum(jnp.sum(equation_misfit * equation_misfit), ('blk', 'sub'))]
    unnamed x2 -> x0, waiting for transfers between devices: 166 us -> none
    ppermute x38 -> x0, starting transfers between devices: 140 us -> none  [the longest x19 87.4 us: extended(): lax.ppermute(lax.slice_in_dim(block, 0, width, axis=dim), axis, backward)]
    pallas_call x0 -> x1, Pallas kernels: none -> 44.8 us  [shards(): pl.pallas_call(kernel, out_shape=(jax.ShapeDtypeStruct((5, 4, 32, 128), F...]
    all_gather x1 -> x0, blocking collectives: 44.5 us -> none  [shards(): lax.all_gather(surface_kelvin, ('blk', 'sub'), axis=0, tiled=True)]
  transfers between devices with their start and end apart: 39 -> 0, of which waited for: 11 -> 0; matrix products, arithmetic and copies ran while one was open for 2% -> 0% of each run, Pallas kernels for 0% -> 0%
where the time goes in v1:
time: 53.5 us; the launch traced here: 53.1 us
  Pallas kernels  44.8 us (84%)
  local copies, waits for them, and re-layouts  7.69 us (14%)
  between operations  0.66 us (1%)
    pallas_call x1, Pallas kernels, shards(): pl.pallas_call(kernel, out_shape=(jax.ShapeDtypeStruct((5, 4, 32, 128), F...  44.8 us
    unnamed x18, local copies, waits for them, and re-layouts  7.69 us

profile of v1, /device:TPU:1, one launch (start us, length us, event | category | flops | bytes accessed | tf_op | source)
XLA Modules:
  0.0 53.1 jit_solution(6456719785266703195)
XLA Ops:
  0.6 0.0 copy-start
  0.6 0.9 %copy-done = f32[3,4,32,128]{3,2,1,0:T(8,128)S(1)} copy-done((f32[3,4,32,128]{3,2,1,0:T(8,128)S(1)}, f32[3,4,32,128]{3,2,1,0:T(8,128)}, u32[]{:S(2)}) %copy-start) | copy-done | bytes 196632
  1.6 0.0 copy-start.1
  1.6 0.9 %copy-done.1 = f32[6,8,8,128]{3,2,1,0:T(8,128)S(1)} copy-done((f32[6,8,8,128]{3,2,1,0:T(8,128)S(1)}, f32[6,8,8,128]{3,2,1,0:T(8,128)}, u32[]{:S(2)}) %copy-start.1) | copy-done | bytes 196632
  2.5 0.0 copy-start.2
  2.5 0.8 %copy-done.2 = f32[4,32,128]{2,1,0:T(8,128)S(1)} copy-done((f32[4,32,128]{2,1,0:T(8,128)S(1)}, f32[4,32,128]{2,1,0:T(8,128)}, u32[]{:S(2)}) %copy-start.2) | copy-done | bytes 65560
  3.3 0.0 copy-start.3
  3.3 0.8 %copy-done.3 = f32[4,32,128]{2,1,0:T(8,128)S(1)} copy-done((f32[4,32,128]{2,1,0:T(8,128)S(1)}, f32[4,32,128]{2,1,0:T(8,128)}, u32[]{:S(2)}) %copy-start.3) | copy-done | bytes 65560
  4.2 0.0 copy-start.4
  4.2 0.8 %copy-done.4 = f32[8,8,128]{2,1,0:T(8,128)S(1)} copy-done((f32[8,8,128]{2,1,0:T(8,128)S(1)}, f32[8,8,128]{2,1,0:T(8,128)}, u32[]{:S(2)}) %copy-start.4) | copy-done | bytes 32792
  4.9 0.0 copy-start.5
  4.9 0.8 %copy-done.5 = s32[8,8,128]{2,1,0:T(8,128)S(1)} copy-done((s32[8,8,128]{2,1,0:T(8,128)S(1)}, s32[8,8,128]{2,1,0:T(8,128)}, u32[]{:S(2)}) %copy-start.5) | copy-done | bytes 32792
  5.7 0.0 copy-start.6
  5.7 0.7 %copy-done.6 = s32[1,1,32]{2,1,0:T(1,128)S(1)} copy-done((s32[1,1,32]{2,1,0:T(1,128)S(1)}, s32[1,1,32]{2,1,0:T(1,128)}, u32[]{:S(2)}) %copy-start.6) | copy-done | bytes 152
  6.3 0.0 copy-start.7
  6.3 0.7 %copy-done.7 = f32[8]{0:T(128)S(1)} copy-done((f32[8]{0:T(128)S(1)}, f32[8]{0:T(128)}, u32[]{:S(2)}) %copy-start.7) | copy-done | bytes 56
  7.0 44.8 %shard_map.95 = (f32[5,4,32,128]{3,2,1,0:T(8,128)S(1)}, f32[8,8,128]{2,1,0:T(8,128)S(1)}) custom-call(f32[4,32,128]{2,1,0:T(8,128)S(1)} %copy-done.2, f32[3,4,32,128]{3,2,1,0:T(8,128)S(1)} %copy-done, f32[4,32,128]{2,1,0:T(8,128)S(1)} %copy-done.3, s32[1,1,32]{2,1,0:T(1,128)S(1)} %copy-done.6, f32[8,8,128]{2,1,0:T(8,128)S(1)} %copy-done.4, ...), custom_call_target="tpu_custom_call" | custom-call | tf_op jit(solution)/shard_map/pallas_call | solution.py:513
  51.8 0.7 %copy.12 = f32[5,4,32,128]{3,2,1,0:T(8,128)} copy(f32[5,4,32,128]{3,2,1,0:T(8,128)S(1)} %get-tuple-element.4) | data formatting | bytes 655360
  52.5 0.6 %copy.13 = f32[8,8,128]{2,1,0:T(8,128)} copy(f32[8,8,128]{2,1,0:T(8,128)S(1)} %get-tuple-element.5) | data formatting | bytes 65536
Async XLA Ops:
  0.6 0.9 %copy-start = (f32[3,4,32,128]{3,2,1,0:T(8,128)S(1)}, f32[3,4,32,128]{3,2,1,0:T(8,128)}, u32[]{:S(2)}) copy-start(f32[3,4,32,128]{3,2,1,0:T(8,128)} %vel_ref.1) | copy-start | bytes 589828
  1.6 0.9 %copy-start.1 = (f32[6,8,8,128]{3,2,1,0:T(8,128)S(1)}, f32[6,8,8,128]{3,2,1,0:T(8,128)}, u32[]{:S(2)}) copy-start(f32[6,8,8,128]{3,2,1,0:T(8,128)} %fc_ref.1) | copy-start | bytes 589828
  2.5 0.8 %copy-start.2 = (f32[4,32,128]{2,1,0:T(8,128)S(1)}, f32[4,32,128]{2,1,0:T(8,128)}, u32[]{:S(2)}) copy-start(f32[4,32,128]{2,1,0:T(8,128)} %rho_ref.1) | copy-start | bytes 196612
  3.3 0.8 %copy-start.3 = (f32[4,32,128]{2,1,0:T(8,128)S(1)}, f32[4,32,128]{2,1,0:T(8,128)}, u32[]{:S(2)}) copy-start(f32[4,32,128]{2,1,0:T(8,128)} %p_ref.1) | copy-start | bytes 196612
  4.2 0.8 %copy-start.4 = (f32[8,8,128]{2,1,0:T(8,128)S(1)}, f32[8,8,128]{2,1,0:T(8,128)}, u32[]{:S(2)}) copy-start(f32[8,8,128]{2,1,0:T(8,128)} %x0_ref.1) | copy-start | bytes 98308
  4.9 0.8 %copy-start.5 = (s32[8,8,128]{2,1,0:T(8,128)S(1)}, s32[8,8,128]{2,1,0:T(8,128)}, u32[]{:S(2)}) copy-start(s32[8,8,128]{2,1,0:T(8,128)} %mat_ref.1) | copy-start | bytes 98308
  5.7 0.7 %copy-start.6 = (s32[1,1,32]{2,1,0:T(1,128)S(1)}, s32[1,1,32]{2,1,0:T(1,128)}, u32[]{:S(2)}) copy-start(s32[1,1,32]{2,1,0:T(1,128)} %idx_ref.1) | copy-start | bytes 388
  6.3 0.7 %copy-start.7 = (f32[8]{0:T(128)S(1)}, f32[8]{0:T(128)}, u32[]{:S(2)}) copy-start(f32[8]{0:T(128)} %cap_ref.1) | copy-start | bytes 100

commit v2 on v1

--- a/solution.py
+++ b/solution.py
@@ -41,11 +41,12 @@
 
 
 def kernel(
-    rho_ref, vel_ref, p_ref, idx_ref, x0_ref, fc_ref, mat_ref, cap_ref,
+    rho_hbm, vel_hbm, p_hbm, idx_hbm, x0_hbm, fc_hbm, mat_hbm, cap_hbm,
     fluid_ref, metal_ref,
+    rho_ref, vel_ref, p_ref, idx_ref, x0_ref, fc_ref, mat_ref, cap_ref, load,
     us, pr, hz, yp, yr, zp, zr, sink, ft,
-    rb1, rw, hc, rhc, wb, rwb,
-    fm, pk_lo, pk_hi, rl, rh, wm, fr, qk_lo, qk_hi, ql, qh, vk, mom, rmom,
+    rb1, rw, ht, hc, rhc, wb, rwb,
+    fm, pk_lo, pk_hi, rl, rh, wm, wu, fr, qk_lo, qk_hi, ql, qh, vk, mom, rmom,
     b1_s, b1_r, y1_s, y1_r, y2_s, y2_r, b2_s, b2_r, fs, frv, ms, mr, rs, rr_, as_, ar,
 ):
     me_g = lax.axis_index("grp")
@@ -73,6 +74,14 @@
     for d in partners:
         pl.semaphore_signal(barrier, inc=1, device_id=d, device_id_type=ID)
 
+    pairs = (
+        (idx_hbm, idx_ref), (p_hbm, p_ref), (rho_hbm, rho_ref), (x0_hbm, x0_ref), (vel_hbm, vel_ref),
+        (cap_hbm, cap_ref), (mat_hbm, mat_ref), (fc_hbm, fc_ref),
+    )
+    loads = [pltpu.make_async_copy(a, b, load.at[n]) for n, (a, b) in enumerate(pairs)]
+    for c in loads:
+        c.start()
+
     def rcopy(src, dst, s, r, dev):
         return pltpu.make_async_remote_copy(
             src_ref=src, dst_ref=dst, send_sem=s, recv_sem=r, device_id=dev, device_id_type=ID
@@ -82,44 +91,8 @@
     sub8 = lax.broadcasted_iota(jnp.int32, (8, 128), 0)
     low4 = sub8 < 4
 
-    def start_x(x, _):
-        rho = rho_ref[x]
-        v = [vel_ref[k, x] for k in range(3)]
-        mo = [rho * a for a in v]
-        us[0, 0, 1 + x, 8:40, :] = rho
-        for k in range(3):
-            us[0, 1 + k, 1 + x, 8:40, :] = mo[k]
-        us[0, 4, 1 + x, 8:40, :] = p_ref[x] / GM1 + 0.5 * (
-            mo[0] * v[0] + mo[1] * v[1] + mo[2] * v[2]
-        )
-        return 0
-
-    lax.fori_loop(0, 4, start_x, 0)
-
-    def pack_fluid(st):
-        lane = lax.broadcasted_iota(jnp.int32, (32, 128), 1)
-        acc = jnp.zeros((32, 128), F32)
-        for x in range(4):
-            for f in range(5):
-                j = x * 5 + f
-                yp[st, 0, j : j + 1, :] = us[st, f, 1 + x, 8:9, :]
-                yp[st, 1, j : j + 1, :] = us[st, f, 1 + x, 39:40, :]
-                tile = pltpu.roll(us[st, f, 1 + x, 8:40, :], 2 * j + 1, 1)
-                acc = jnp.where((lane == 2 * j) | (lane == 2 * j + 1), tile, acc)
-        zp[st] = acc
-
-    def fluid_copies(st):
-        rows = pl.ds(8, 32)
-        return [
-            rcopy(us.at[st, :, 1, rows, :], us.at[st, :, 5, rows, :], fs.at[st, 0], frv.at[st, 0], {"blk": blk(-1)}),
-            rcopy(us.at[st, :, 4, rows, :], us.at[st, :, 0, rows, :], fs.at[st, 1], frv.at[st, 1], {"blk": blk(1)}),
-            rcopy(yp.at[st, 0], yr.at[st, 1], fs.at[st, 2], frv.at[st, 2], {"sub": sub(-1)}),
-            rcopy(yp.at[st, 1], yr.at[st, 0], fs.at[st, 3], frv.at[st, 3], {"sub": sub(1)}),
-            rcopy(zp.at[st], zr.at[st, 0], fs.at[st, 4], frv.at[st, 4], zhi),
-            rcopy(zp.at[st], zr.at[st, 1], fs.at[st, 5], frv.at[st, 5], zlo),
-        ]
-
-    pack_fluid(0)
+    for c in loads[0:3]:
+        c.wait()
 
     idx = idx_ref[0]
     dev_of = lax.shift_right_logical(idx, 3)
@@ -134,6 +107,55 @@
     for m in range(8):
         ft[m, 0] = by_dev[8 * m : 8 * m + 8]
         ft[m, 1] = slot_rows[8 * m : 8 * m + 8]
+    ft[8] = ft[0]
+
+    rb1[me_b] = ft[pl.ds(me_b, 2)]
+    loads[3].wait()
+    rw[me_s] = x0_ref[0]
+    loads[4].wait()
+
+    def start_x(x, _):
+        rho = rho_ref[x]
+        v = [vel_ref[k, x] for k in range(3)]
+        mo = [rho * a for a in v]
+        us[0, 0, 1 + x, 8:40, :] = rho
+        for k in range(3):
+            us[0, 1 + k, 1 + x, 8:40, :] = mo[k]
+        us[0, 4, 1 + x, 8:40, :] = p_ref[x] / GM1 + 0.5 * (
+            mo[0] * v[0] + mo[1] * v[1] + mo[2] * v[2]
+        )
+        return 0
+
+    for x in range(4):
+        start_x(x, 0)
+
+    def pack_fluid(st):
+        lane = lax.broadcasted_iota(jnp.int32, (32, 128), 1)
+        acc = jnp.zeros((32, 128), F32)
+        for x in range(4):
+            for f in range(5):
+                j = x * 5 + f
+                yp[st, 0, j : j + 1, :] = us[st, f, 1 + x, 8:9, :]
+                yp[st, 1, j : j + 1, :] = us[st, f, 1 + x, 39:40, :]
+                tile = pltpu.roll(us[st, f, 1 + x, 8:40, :], 2 * j + 1, 1)
+                acc = jnp.where((lane == 2 * j) | (lane == 2 * j + 1), tile, acc)
+        zp[st] = acc
+
+    def fluid_copies(st):
+        rows = pl.ds(8, 32)
+        return [
+            rcopy(us.at[st, :, 1, rows, :], us.at[st, :, 5, rows, :], fs.at[st, 0], frv.at[st, 0], {"blk": blk(-1)}),
+            rcopy(us.at[st, :, 4, rows, :], us.at[st, :, 0, rows, :], fs.at[st, 1], frv.at[st, 1], {"blk": blk(1)}),
+            rcopy(yp.at[st, 0], yr.at[st, 1], fs.at[st, 2], frv.at[st, 2], {"sub": sub(-1)}),
+            rcopy(yp.at[st, 1], yr.at[st, 0], fs.at[st, 3], frv.at[st, 3], {"sub": sub(1)}),
+            rcopy(zp.at[st], zr.at[st, 0], fs.at[st, 4], frv.at[st, 4], zhi),
+            rcopy(zp.at[st], zr.at[st, 1], fs.at[st, 5], frv.at[st, 5], zlo),
+        ]
+
+    pack_fluid(0)
+
+    for c in loads[5:8]:
+        c.wait()
 
     for x in range(8):
         mat = mat_ref[x]
@@ -171,14 +193,11 @@
             rcopy(cut(lo, 0, 2), cut(dh, 6, 8), s.at[7], r.at[7], {"blk": blk(-1), "sub": sub(-1)}),
         ]
 
-    rb1[me_b] = ft[me_b]
-    rw[me_s] = x0_ref[0]
-
     pl.semaphore_wait(barrier, len(partners))
 
     for k in range(1, nb):
         to = blk(k)
-        rcopy(ft.at[to], rb1.at[me_b], b1_s, b1_r, {"blk": to}).start()
+        rcopy(ft.at[pl.ds(to, 2)], rb1.at[me_b], b1_s, b1_r, {"blk": to}).start()
     for k in range(1, nsub):
         rcopy(x0_ref.at[0], rw.at[me_s], y1_s, y1_r, {"sub": sub(k)}).start()
     halo = [fluid_copies(st) for st in range(3)]
@@ -194,11 +213,8 @@
             pr[k, x, r0 : r0 + n, :] = val
 
     def own_prims(st):
-        def body(x, _):
+        for x in range(1, 5):
             prims_at(st, x, 8, 32)
-            return 0
-
-        lax.fori_loop(1, 5, body, 0)
 
     def halo_in(st):
         for c in halo[st]:
@@ -213,18 +229,15 @@
         lane = lax.broadcasted_iota(jnp.int32, (32, 128), 1)
         both = jnp.where((lane & 1) == 0, zr[st, 0], pltpu.roll(zr[st, 1], 126, 1))
 
-        def body(x, _):
+        for x in range(4):
             prims_at(st, 1 + x, 0, 8)
             prims_at(st, 1 + x, 40, 8)
-            u = [pltpu.roll(both, 128 - 2 * (x * 5 + f), 1) for f in range(5)]
+            u = [pltpu.roll(both, (128 - 2 * (x * 5 + f)) % 128, 1) for f in range(5)]
             q = primitives(u)
             for f in range(5):
                 hz[f, x] = u[f]
             for f, val in enumerate((q[2], q[3], q[4])):
                 hz[5 + f, x] = val
-            return 0
-
-        lax.fori_loop(0, 4, body, 0)
 
     def stage(st, with_sink):
         first, last = lane8 == 0, lane8 == 127
@@ -284,21 +297,32 @@
 
     wait_all(rb1.at[0:7], b1_s, b1_r, near_b).wait_recv()
 
+    want = (sub8 + 1).astype(F32)
+
     def gather_strips(m, _):
-        total = jnp.zeros((8, 128), F32)
-        count = jnp.zeros((8, 128), F32)
-        want = (sub8 + 1).astype(F32)
-        for b in range(8):
-            val = jnp.broadcast_to(rb1[b, 0, pl.ds(m, 1), :], (8, 128))
-            slot = jnp.broadcast_to(rb1[b, 1, pl.ds(m, 1), :], (8, 128))
-            here = slot == want
-            total = total + jnp.where(here, val, 0.0)
-            count = count + jnp.where(here, 1.0, 0.0)
-        hc[m, 0] = total
-        hc[m, 1] = count
+        for o in range(2):
+            total = jnp.zeros((8, 128), F32)
+            count = jnp.zeros((8, 128), F32)
+            for b in range(8):
+                val = jnp.broadcast_to(rb1[b, o, 0, pl.ds(m, 1), :], (8, 128))
+                slot = jnp.broadcast_to(rb1[b, o, 1, pl.ds(m, 1), :], (8, 128))
+                here = slot == want
+                total = total + jnp.where(here, val, 0.0)
+                count = count + jnp.where(here, 1.0, 0.0)
+            ht[m, o, 0] = pltpu.roll(total, 4, 0)
+            ht[m, o, 1] = pltpu.roll(count, 4, 0)
         return 0
 
     lax.fori_loop(0, 8, gather_strips, 0)
+    for m in range(8):
+        counts = jnp.zeros((8, 128), F32)
+        for o in range(2):
+            for t, (a, b) in enumerate((((m + 7) % 8, m), (m, (m + 1) % 8))):
+                hc[m, 2 * o + t] = jnp.where(low4, ht[a, o, 0], ht[b, o, 0])
+                counts = jnp.where(
+                    lane8 == 2 * o + t, jnp.where(low4, ht[a, o, 1], ht[b, o, 1]), counts
+                )
+        hc[m, 4] = counts
     rhc[me_s] = hc[me_s]
     for k in range(1, nsub):
         to = sub(k)
@@ -306,7 +330,7 @@
 
     wait_all(rw.at[0:7], y1_s, y1_r, near_s).wait_recv()
     walls = jnp.concatenate([rw[m] for m in range(8)], axis=0)
-    slots = jnp.concatenate([rb1[b, 1] for b in range(8)], axis=0)[:, 0:64]
+    slots = jnp.concatenate([rb1[b, 0, 1] for b in range(8)], axis=0)[:, 0:64]
     row = lax.broadcasted_iota(jnp.int32, (64, 64), 0)
     col = lax.broadcasted_iota(jnp.int32, (64, 64), 1)
     pick = (lax.shift_right_logical(col, 3) == (row & 7)) & (((col & 7) + 1).astype(F32) == slots)
@@ -319,6 +343,45 @@
     for k in range(1, nb):
         to = blk(k)
         rcopy(wb.at[to], rwb.at[me_b], b2_s, b2_r, {"blk": to}).start()
+
+    for c in coarse:
+        c.wait_recv()
+
+    def window(x, mid, lo, hi, odd):
+        turned = pltpu.roll(mid, 4, 0)
+        if odd:
+            lo = pltpu.roll(lo, 4, 0)
+        else:
+            hi = pltpu.roll(hi, 4, 0)
+        return jnp.where(low4, lo, turned), jnp.where(low4, turned, hi)
+
+    def build(f, _):
+        for x in range(16):
+            w0, w1 = window(x, fm[f, x], rl[f, x // 2], rh[f, x // 2], x % 2)
+            wm[f, x, 0:8, :] = w0
+            wm[f, x, 8:16, :] = w1
+        return 0
+
+    lax.fori_loop(0, 5, build, 0)
+    for x in range(1, 15):
+        wu[0, x] = pltpu.roll(wm[3, x], 15, 0)
+        wu[1, x] = pltpu.roll(wm[4, x], 127, 1)
+
+    def laplace(x):
+        v = wm[0, x]
+        ky, kz = wm[3, x], wm[4, x]
+        gy = ky * (v - pltpu.roll(v, 1, 0))
+        gz = kz * (v - pltpu.roll(v, 1, 1))
+        out = wm[2, x] * (v - wm[0, x - 1]) + wm[2, x + 1] * (v - wm[0, x + 1])
+        return out + (gy - pltpu.roll(gy, 15, 0)) + (gz - pltpu.roll(gz, 127, 1))
+
+    for x in range(8):
+        lap = laplace(4 + x)
+        fr[0, 4 + x] = pltpu.roll(jnp.where(low4, lap[8:16], lap[0:8]), 4, 0) * (-WIDTH)
+    pack_metal(lambda x: fr[0, 4 + x], qk_lo.at[0], qk_hi.at[0])
+    fine = metal_copies(fr, qk_lo, qk_hi, ql, qh, rs, rr_)
+    for c in fine:
+        c.start()
 
     halo_in(0)
     stage(0, False)
@@ -342,61 +405,7 @@
     pack_fluid(1)
     for c in halo[1]:
         c.start()
-
-    for c in coarse:
-        c.wait_recv()
-
-    def window(x, mid, lo, hi, odd):
-        turned = pltpu.roll(mid, 4, 0)
-        if odd:
-            lo = pltpu.roll(lo, 4, 0)
-        else:
-            hi = pltpu.roll(hi, 4, 0)
-        return jnp.where(low4, lo, turned), jnp.where(low4, turned, hi)
-
-    def build(f, _):
-        for x in range(16):
-            w0, w1 = window(x, fm[f, x], rl[f, x // 2], rh[f, x // 2], x % 2)
-            wm[f, x, 0:8, :] = w0
-            wm[f, x, 8:16, :] = w1
-        return 0
-
-    lax.fori_loop(0, 5, build, 0)
-
-    def laplace(x):
-        v = wm[0, x]
-        ky, kz = wm[3, x], wm[4, x]
-        gy = ky * (v - pltpu.roll(v, 1, 0))
-        gz = kz * (v - pltpu.roll(v, 1, 1))
-        out = wm[2, x] * (v - wm[0, x - 1]) + wm[2, x + 1] * (v - wm[0, x + 1])
-        return out + (gy - pltpu.roll(gy, 15, 0)) + (gz - pltpu.roll(gz, 127, 1))
-
-    wait_all(rhc.at[0:7], y2_s, y2_r, near_s).wait_recv()
-    total = rhc[0, 0]
-    count = rhc[0, 1]
-    for m in range(1, 8):
-        total = total + rhc[m, 0]
-        count = count + rhc[m, 1]
-    heat_in = total - count * x0_ref[0]
-
-    def start_r(x, _):
-        lap = laplace(4 + x)
-        fr[0, 4 + x] = pltpu.roll(jnp.where(low4, lap[8:16], lap[0:8]), 4, 0) * (-WIDTH)
-        return 0
-
-    lax.fori_loop(0, 8, start_r, 0)
-    fr[0, 4] = fr[0, 4] + heat_in
-    pack_metal(lambda x: fr[0, 4 + x], qk_lo.at[0], qk_hi.at[0])
-    fine = metal_copies(fr, qk_lo, qk_hi, ql, qh, rs, rr_)
-    for c in fine:
-        c.start()
-
     own_prims(1)
-    halo_in(1)
-    stage(1, True)
-    pack_fluid(2)
-    for c in halo[2]:
-        c.start()
 
     for c in fine:
         c.wait_recv()
@@ -404,25 +413,32 @@
         w0, w1 = window(x, fr[0, x], ql[0, x // 2], qh[0, x // 2], x % 2)
         vk[0, x, 0:8, :] = w0
         vk[0, x, 8:16, :] = w1
+    wait_all(rhc.at[0:7], y2_s, y2_r, near_s).wait_recv()
+    arrived = []
+    for t in range(5):
+        total = rhc[0, t]
+        for m in range(1, 8):
+            total = total + rhc[m, t]
+        arrived.append(total)
+    for o, x in ((0, 4), (1, 12)):
+        for t in range(2):
+            count = jnp.sum(jnp.where(lane8 == 2 * o + t, arrived[4], 0.0), axis=1, keepdims=True)
+            rows = slice(8 * t, 8 * t + 8)
+            vk[0, x, rows, :] = vk[0, x, rows, :] + (arrived[2 * o + t] - count * wm[0, x, rows, :])
 
     for n in range(4):
 
-        def apply(x, _):
+        for x in range(n + 1, 15 - n):
             v = vk[n, x]
-            ky, kz = wm[3, x], wm[4, x]
             out = wm[1, x] * v - wm[2, x] * vk[n, x - 1] - wm[2, x + 1] * vk[n, x + 1]
-            out = out - ky * pltpu.roll(v, 1, 0) - pltpu.roll(ky, 15, 0) * pltpu.roll(v, 15, 0)
-            out = out - kz * pltpu.roll(v, 1, 1) - pltpu.roll(kz, 127, 1) * pltpu.roll(v, 127, 1)
+            out = out - wm[3, x] * pltpu.roll(v, 1, 0) - wu[0, x] * pltpu.roll(v, 15, 0)
+            out = out - wm[4, x] * pltpu.roll(v, 1, 1) - wu[1, x] * pltpu.roll(v, 127, 1)
             vk[n + 1, x] = out
-            return 0
-
-        lax.fori_loop(n + 1, 15 - n, apply, 0)
-
-    def dots(x, acc):
+
+    acc = [jnp.zeros((8, 128), F32) for _ in range(8)]
+    for x in range(4, 12):
         v = [vk[n, x, 4:12, :] for n in range(5)]
-        return tuple(a + v[k // 2] * v[(k + 1) // 2] for k, a in enumerate(acc))
-
-    acc = lax.fori_loop(4, 12, dots, tuple(jnp.zeros((8, 128), F32) for _ in range(8)))
+        acc = [a + v[k // 2] * v[(k + 1) // 2] for k, a in enumerate(acc)]
     tile = jnp.zeros((8, 128), F32)
     for k in range(8):
         tile = jnp.where(sub8 == k, jnp.sum(acc[k], axis=0, keepdims=True), tile)
@@ -440,6 +456,12 @@
         return 0
 
     lax.fori_loop(1, 64, send_moments, 0)
+
+    halo_in(1)
+    stage(1, True)
+    pack_fluid(2)
+    for c in halo[2]:
+        c.start()
 
     own_prims(2)
     halo_in(2)
@@ -516,16 +538,18 @@
             jax.ShapeDtypeStruct((5, 4, 32, 128), F32),
             jax.ShapeDtypeStruct((8, 8, 128), F32),
         ),
-        in_specs=[vmem] * 7 + [pl.BlockSpec(memory_space=pltpu.SMEM)],
+        in_specs=[pl.BlockSpec(memory_space=pltpu.HBM)] * 8,
         out_specs=(vmem, vmem),
         scratch_shapes=[
+            buf(4, 32, 128), buf(3, 4, 32, 128), buf(4, 32, 128), pltpu.VMEM((1, 1, 32), jnp.int32),
+            buf(8, 8, 128), buf(6, 8, 8, 128), pltpu.VMEM((8, 8, 128), jnp.int32), pltpu.SMEM((8,), F32), dma((8,)),
             buf(3, 5, 6, 48, 128), buf(5, 6, 48, 128), buf(8, 4, 32, 128),
             buf(3, 2, 24, 128), buf(3, 2, 24, 128), buf(3, 32, 128), buf(3, 2, 32, 128),
-            buf(4, 32, 128), buf(8, 2, 8, 128),
-            buf(8, 2, 8, 128), buf(8, 8, 128), buf(8, 2, 8, 128), buf(8, 2, 8, 128),
+            buf(4, 32, 128), buf(9, 2, 8, 128),
+            buf(8, 2, 2, 8, 128), buf(8, 8, 128), buf(8, 2, 2, 8, 128), buf(8, 5, 8, 128), buf(8, 5, 8, 128),
             buf(8, 8, 128), buf(8, 8, 128),
             buf(5, 16, 8, 128), buf(5, 4, 8, 128), buf(5, 4, 8, 128),
-            buf(5, 8, 8, 128), buf(5, 8, 8, 128), buf(5, 16, 16, 128),
+            buf(5, 8, 8, 128), buf(5, 8, 8, 128), buf(5, 16, 16, 128), buf(2, 16, 16, 128),
             buf(1, 16, 8, 128), buf(1, 4, 8, 128), buf(1, 4, 8, 128),
             buf(1, 8, 8, 128), buf(1, 8, 8, 128), buf(5, 16, 16, 128),
             buf(1, 128), buf(64, 1, 128),
@@ -533,7 +557,7 @@
             dma((3, 6)), dma((3, 6)), dma((8,)), dma((8,)), dma((8,)), dma((8,)), dma, dma,
         ],
         compiler_params=pltpu.CompilerParams(
-            collective_id=0, has_side_effects=True, vmem_limit_bytes=32 * 1024 * 1024
+            collective_id=0, has_side_effects=True, vmem_limit_bytes=56 * 1024 * 1024
         ),
     )(rho, vel, p, idx, x0, fc, mat, cap)
 

time: 53.5 us -> 42.6 us (0.80)
  Pallas kernels: 44.8 us -> 39.4 us
  local copies, waits for them, and re-layouts: 7.69 us -> 2.35 us
    pallas_call x1, Pallas kernels: 44.8 us -> 39.4 us  [shards(): pl.pallas_call(kernel, out_shape=(jax.ShapeDtypeStruct((5, 4, 32, 128), F...]
    unnamed x18 -> x4, local copies, waits for them, and re-layouts: 7.69 us -> 2.35 us
where the time goes in v2:
time: 42.6 us; the launch traced here: 42.4 us
  Pallas kernels  39.4 us (92%)
  local copies, waits for them, and re-layouts  2.35 us (6%)
  between operations  0.65 us (2%)
    pallas_call x1, Pallas kernels, shards(): pl.pallas_call(kernel, out_shape=(jax.ShapeDtypeStruct((5, 4, 32, 128), F...  39.4 us
    unnamed x4, local copies, waits for them, and re-layouts  2.35 us

profile of v2, /device:TPU:1, one launch (start us, length us, event | category | flops | bytes accessed | tf_op | source)
XLA Modules:
  0.0 42.4 jit_solution(14218853152835016778)
XLA Ops:
  0.6 39.4 %shard_map.95 = (f32[5,4,32,128]{3,2,1,0:T(8,128)}, f32[8,8,128]{2,1,0:T(8,128)}) custom-call(f32[4,32,128]{2,1,0:T(8,128)} %rho_hbm.1, f32[3,4,32,128]{3,2,1,0:T(8,128)} %vel_hbm.1, f32[4,32,128]{2,1,0:T(8,128)} %p_hbm.1, s32[1,1,32]{2,1,0:T(1,128)} %idx_hbm.1, f32[8,8,128]{2,1,0:T(8,128)} %x0_hbm.1, f32[6,8,8,128]{3,2,1,0:T(8,128)} %fc_hbm.1, ...), custom_call_target="tpu_custom_call" | custom-call | tf_op jit(solution)/shard_map/pallas_call | solution.py:535
  40.1 0.0 copy-start
  40.1 1.7 %copy.12 = f32[5,4,32,128]{3,2,1,0:T(8,128)} copy(f32[5,4,32,128]{3,2,1,0:T(8,128)} %get-tuple-element.4) | data formatting | bytes 655360
  41.8 0.0 copy-done
  41.8 0.6 %copy.13 = f32[8,8,128]{2,1,0:T(8,128)} copy(f32[8,8,128]{2,1,0:T(8,128)S(1)} %copy-done) | data formatting | bytes 65536
Async XLA Ops:
  40.1 1.7 %copy-start = (f32[8,8,128]{2,1,0:T(8,128)S(1)}, f32[8,8,128]{2,1,0:T(8,128)}, u32[]{:S(2)}) copy-start(f32[8,8,128]{2,1,0:T(8,128)} %get-tuple-element.5) | copy-start | bytes 98308

commit v3 on v2

--- a/solution.py
+++ b/solution.py
@@ -42,8 +42,9 @@
 
 def kernel(
     rho_hbm, vel_hbm, p_hbm, idx_hbm, x0_hbm, fc_hbm, mat_hbm, cap_hbm,
-    fluid_ref, metal_ref,
+    fluid_hbm, metal_hbm,
     rho_ref, vel_ref, p_ref, idx_ref, x0_ref, fc_ref, mat_ref, cap_ref, load,
+    fluid_ref, metal_ref, store,
     us, pr, hz, yp, yr, zp, zr, sink, ft,
     rb1, rw, ht, hc, rhc, wb, rwb,
     fm, pk_lo, pk_hi, rl, rh, wm, wu, fr, qk_lo, qk_hi, ql, qh, vk, mom, rmom,
@@ -66,8 +67,10 @@
         return lax.rem(me_g + (k + ng), ng)
 
     zlo, zhi = {"grp": grp(-1)}, {"grp": grp(1)}
-    partners = [{"blk": blk(k)} for k in range(1, nb)]
-    partners += [{"sub": sub(k)} for k in range(1, nsub)]
+    far_s = (4, 3, 5, 2, 6, 1, 7)
+    far_b = (4, 5, 3, 2, 6, 7, 1)
+    partners = [{"blk": blk(k)} for k in far_b]
+    partners += [{"sub": sub(k)} for k in far_s]
     partners += [zlo, zhi]
     partners += [{"blk": blk(i), "sub": sub(j)} for i in (-1, 1) for j in (-1, 1)]
     barrier = pltpu.get_barrier_semaphore()
@@ -112,6 +115,13 @@
     rb1[me_b] = ft[pl.ds(me_b, 2)]
     loads[3].wait()
     rw[me_s] = x0_ref[0]
+
+    pl.semaphore_wait(barrier, len(partners))
+    for k in far_s:
+        rcopy(x0_ref.at[0], rw.at[me_s], y1_s, y1_r, {"sub": sub(k)}).start()
+    for k in far_b:
+        to = blk(k)
+        rcopy(ft.at[pl.ds(to, 2)], rb1.at[me_b], b1_s, b1_r, {"blk": to}).start()
     loads[4].wait()
 
     def start_x(x, _):
@@ -144,8 +154,9 @@
     def fluid_copies(st):
         rows = pl.ds(8, 32)
         return [
-            rcopy(us.at[st, :, 1, rows, :], us.at[st, :, 5, rows, :], fs.at[st, 0], frv.at[st, 0], {"blk": blk(-1)}),
             rcopy(us.at[st, :, 4, rows, :], us.at[st, :, 0, rows, :], fs.at[st, 1], frv.at[st, 1], {"blk": blk(1)}),
+            rcopy(us.at[st, 0:4, 1, rows, :], us.at[st, 0:4, 5, rows, :], fs.at[st, 0], frv.at[st, 0], {"blk": blk(-1)}),
+            rcopy(us.at[st, 4, 1, rows, :], us.at[st, 4, 5, rows, :], fs.at[st, 6], frv.at[st, 6], {"blk": blk(-1)}),
             rcopy(yp.at[st, 0], yr.at[st, 1], fs.at[st, 2], frv.at[st, 2], {"sub": sub(-1)}),
             rcopy(yp.at[st, 1], yr.at[st, 0], fs.at[st, 3], frv.at[st, 3], {"sub": sub(1)}),
             rcopy(zp.at[st], zr.at[st, 0], fs.at[st, 4], frv.at[st, 4], zhi),
@@ -153,6 +164,9 @@
         ]
 
     pack_fluid(0)
+    halo = [fluid_copies(st) for st in range(3)]
+    for c in halo[0]:
+        c.start()
 
     for c in loads[5:8]:
         c.wait()
@@ -193,19 +207,14 @@
             rcopy(cut(lo, 0, 2), cut(dh, 6, 8), s.at[7], r.at[7], {"blk": blk(-1), "sub": sub(-1)}),
         ]
 
-    pl.semaphore_wait(barrier, len(partners))
-
-    for k in range(1, nb):
-        to = blk(k)
-        rcopy(ft.at[pl.ds(to, 2)], rb1.at[me_b], b1_s, b1_r, {"blk": to}).start()
-    for k in range(1, nsub):
-        rcopy(x0_ref.at[0], rw.at[me_s], y1_s, y1_r, {"sub": sub(k)}).start()
-    halo = [fluid_copies(st) for st in range(3)]
-    for c in halo[0]:
-        c.start()
     coarse = metal_copies(fm, pk_lo, pk_hi, rl, rh, ms, mr)
     for c in coarse:
         c.start()
+
+    stores = [
+        pltpu.make_async_copy(fluid_ref.at[:, x], fluid_hbm.at[:, x], store.at[x]) for x in range(4)
+    ]
+    stores.append(pltpu.make_async_copy(metal_ref, metal_hbm, store.at[4]))
 
     def prims_at(st, x, r0, n):
         u = [us[st, f, x, r0 : r0 + n, :] for f in range(5)]
@@ -242,7 +251,7 @@
     def stage(st, with_sink):
         first, last = lane8 == 0, lane8 == 127
 
-        def body(x, _):
+        def body(x):
             for t in range(4):
                 r = 8 + 8 * t
 
@@ -283,9 +292,19 @@
                         fluid_ref[f, x, r - 8 : r, :] = new
                     else:
                         us[st + 1, f, 1 + x, r : r + 8, :] = new
-            return 0
-
-        lax.fori_loop(0, 4, body, 0)
+            if st == 2:
+                stores[x].start()
+
+        body(3)
+        if st < 2:
+            halo[st + 1][0].start()
+        body(0)
+        if st < 2:
+            halo[st + 1][1].start()
+        if st == 1:
+            halo[2][2].start()
+        body(1)
+        body(2)
 
     own_prims(0)
 
@@ -324,7 +343,7 @@
                 )
         hc[m, 4] = counts
     rhc[me_s] = hc[me_s]
-    for k in range(1, nsub):
+    for k in far_s:
         to = sub(k)
         rcopy(hc.at[to], rhc.at[me_s], y2_s, y2_r, {"sub": to}).start()
 
@@ -340,7 +359,7 @@
     for b in range(8):
         wb[b] = wall_rows[8 * b : 8 * b + 8]
     rwb[me_b] = wb[me_b]
-    for k in range(1, nb):
+    for k in far_b:
         to = blk(k)
         rcopy(wb.at[to], rwb.at[me_b], b2_s, b2_r, {"blk": to}).start()
 
@@ -402,8 +421,9 @@
     for x in range(1, 4):
         sink[x] = jnp.zeros((32, 128), F32)
     us[1, 4, 1, 8:40, :] = us[1, 4, 1, 8:40, :] - DT * heat_flux
+    halo[1][2].start()
     pack_fluid(1)
-    for c in halo[1]:
+    for c in halo[1][3:]:
         c.start()
     own_prims(1)
 
@@ -447,20 +467,15 @@
     mine = me_b * 8 + me_s
     rmom[mine] = mom[...]
 
-    def send_moments(k, _):
-        to = {
-            "blk": lax.rem(me_b + k // 8, 8),
-            "sub": lax.rem(me_s + k % 8, 8),
-        }
-        rcopy(mom, rmom.at[mine], as_, ar, to).start()
-        return 0
-
-    lax.fori_loop(1, 64, send_moments, 0)
+    for k in far_s + (0,):
+        for j in far_b + (0,):
+            if (j, k) != (0, 0):
+                rcopy(mom, rmom.at[mine], as_, ar, {"blk": blk(j), "sub": sub(k)}).start()
 
     halo_in(1)
     stage(1, True)
     pack_fluid(2)
-    for c in halo[2]:
+    for c in halo[2][3:]:
         c.start()
 
     own_prims(2)
@@ -515,6 +530,7 @@
         for n in range(4):
             out = out + coef[n] * vk[n, 4 + x, 4:12, :]
         metal_ref[x] = out
+    stores[4].start()
 
     wait_all(rb1.at[0:7], b1_s, b1_r, near_b).wait_send()
     wait_all(rw.at[0:7], y1_s, y1_r, near_s).wait_send()
@@ -523,10 +539,11 @@
     for c in halo[0] + halo[1] + halo[2] + coarse + fine:
         c.wait_send()
     wait_all(rmom.at[0:63], as_, ar, near_b).wait_send()
+    for c in stores:
+        c.wait()
 
 
 def shards(rho, vel, p, idx, x0, fc, mat, cap):
-    vmem = pl.BlockSpec(memory_space=pltpu.VMEM)
     dma = pltpu.SemaphoreType.DMA
 
     def buf(*shape):
@@ -539,10 +556,11 @@
             jax.ShapeDtypeStruct((8, 8, 128), F32),
         ),
         in_specs=[pl.BlockSpec(memory_space=pltpu.HBM)] * 8,
-        out_specs=(vmem, vmem),
+        out_specs=(pl.BlockSpec(memory_space=pltpu.HBM),) * 2,
         scratch_shapes=[
             buf(4, 32, 128), buf(3, 4, 32, 128), buf(4, 32, 128), pltpu.VMEM((1, 1, 32), jnp.int32),
             buf(8, 8, 128), buf(6, 8, 8, 128), pltpu.VMEM((8, 8, 128), jnp.int32), pltpu.SMEM((8,), F32), dma((8,)),
+            buf(5, 4, 32, 128), buf(8, 8, 128), dma((5,)),
             buf(3, 5, 6, 48, 128), buf(5, 6, 48, 128), buf(8, 4, 32, 128),
             buf(3, 2, 24, 128), buf(3, 2, 24, 128), buf(3, 32, 128), buf(3, 2, 32, 128),
             buf(4, 32, 128), buf(9, 2, 8, 128),
@@ -554,7 +572,7 @@
             buf(1, 8, 8, 128), buf(1, 8, 8, 128), buf(5, 16, 16, 128),
             buf(1, 128), buf(64, 1, 128),
             dma, dma, dma, dma, dma, dma, dma, dma,
-            dma((3, 6)), dma((3, 6)), dma((8,)), dma((8,)), dma((8,)), dma((8,)), dma, dma,
+            dma((3, 7)), dma((3, 7)), dma((8,)), dma((8,)), dma((8,)), dma((8,)), dma, dma,
         ],
         compiler_params=pltpu.CompilerParams(
             collective_id=0, has_side_effects=True, vmem_limit_bytes=56 * 1024 * 1024

time: 42.6 us -> 41.7 us (0.979)
  Pallas kernels: 39.4 us -> 38.5 us
    pallas_call x1, Pallas kernels: 39.4 us -> 38.5 us  [shards(): pl.pallas_call(kernel, out_shape=(jax.ShapeDtypeStruct((5, 4, 32, 128), F...]
where the time goes in v3:
time: 41.7 us; the launch traced here: 41.5 us
  Pallas kernels  38.5 us (92%)
  local copies, waits for them, and re-layouts  2.35 us (6%)
  between operations  0.65 us (2%)
    pallas_call x1, Pallas kernels, shards(): pl.pallas_call(kernel, out_shape=(jax.ShapeDtypeStruct((5, 4, 32, 128), F...  38.5 us
    unnamed x4, local copies, waits for them, and re-layouts  2.35 us

profile of v3, /device:TPU:1, one launch (start us, length us, event | category | flops | bytes accessed | tf_op | source)
XLA Modules:
  0.0 41.5 jit_solution(12109517143977217482)
XLA Ops:
  0.6 38.5 %shard_map.95 = (f32[5,4,32,128]{3,2,1,0:T(8,128)}, f32[8,8,128]{2,1,0:T(8,128)}) custom-call(f32[4,32,128]{2,1,0:T(8,128)} %rho_hbm.1, f32[3,4,32,128]{3,2,1,0:T(8,128)} %vel_hbm.1, f32[4,32,128]{2,1,0:T(8,128)} %p_hbm.1, s32[1,1,32]{2,1,0:T(1,128)} %idx_hbm.1, f32[8,8,128]{2,1,0:T(8,128)} %x0_hbm.1, f32[6,8,8,128]{3,2,1,0:T(8,128)} %fc_hbm.1, ...), custom_call_target="tpu_custom_call" | custom-call | tf_op jit(solution)/shard_map/pallas_call | solution.py:552
  39.2 0.0 copy-start
  39.2 1.7 %copy.12 = f32[5,4,32,128]{3,2,1,0:T(8,128)} copy(f32[5,4,32,128]{3,2,1,0:T(8,128)} %get-tuple-element.4) | data formatting | bytes 655360
  40.9 0.0 copy-done
  40.9 0.6 %copy.13 = f32[8,8,128]{2,1,0:T(8,128)} copy(f32[8,8,128]{2,1,0:T(8,128)S(1)} %copy-done) | data formatting | bytes 65536
Async XLA Ops:
  39.2 1.7 %copy-start = (f32[8,8,128]{2,1,0:T(8,128)S(1)}, f32[8,8,128]{2,1,0:T(8,128)}, u32[]{:S(2)}) copy-start(f32[8,8,128]{2,1,0:T(8,128)} %get-tuple-element.5) | copy-start | bytes 98308

commit v4 on v3

--- a/solution.py
+++ b/solution.py
@@ -139,12 +139,14 @@
     for x in range(4):
         start_x(x, 0)
 
-    def pack_fluid(st):
+    def pack_fluid(st, part=range(20), more=False):
         lane = lax.broadcasted_iota(jnp.int32, (32, 128), 1)
-        acc = jnp.zeros((32, 128), F32)
+        acc = zp[st] if more else jnp.zeros((32, 128), F32)
         for x in range(4):
             for f in range(5):
                 j = x * 5 + f
+                if j not in part:
+                    continue
                 yp[st, 0, j : j + 1, :] = us[st, f, 1 + x, 8:9, :]
                 yp[st, 1, j : j + 1, :] = us[st, f, 1 + x, 39:40, :]
                 tile = pltpu.roll(us[st, f, 1 + x, 8:40, :], 2 * j + 1, 1)
@@ -332,7 +334,8 @@
             ht[m, o, 1] = pltpu.roll(count, 4, 0)
         return 0
 
-    lax.fori_loop(0, 8, gather_strips, 0)
+    for m in range(8):
+        gather_strips(m, 0)
     for m in range(8):
         counts = jnp.zeros((8, 128), F32)
         for o in range(2):
@@ -347,12 +350,12 @@
         to = sub(k)
         rcopy(hc.at[to], rhc.at[me_s], y2_s, y2_r, {"sub": to}).start()
 
-    wait_all(rw.at[0:7], y1_s, y1_r, near_s).wait_recv()
-    walls = jnp.concatenate([rw[m] for m in range(8)], axis=0)
     slots = jnp.concatenate([rb1[b, 0, 1] for b in range(8)], axis=0)[:, 0:64]
     row = lax.broadcasted_iota(jnp.int32, (64, 64), 0)
     col = lax.broadcasted_iota(jnp.int32, (64, 64), 1)
     pick = (lax.shift_right_logical(col, 3) == (row & 7)) & (((col & 7) + 1).astype(F32) == slots)
+    wait_all(rw.at[0:7], y1_s, y1_r, near_s).wait_recv()
+    walls = jnp.concatenate([rw[m] for m in range(8)], axis=0)
     wall_rows = jnp.dot(
         pick.astype(F32), walls, precision=lax.Precision.HIGHEST, preferred_element_type=F32
     )
@@ -405,24 +408,25 @@
     halo_in(0)
     stage(0, False)
 
-    wait_all(rwb.at[0:7], b2_s, b2_r, near_b).wait_recv()
     lane32 = lax.broadcasted_iota(jnp.int32, (32, 128), 1)
     sub32 = lax.broadcasted_iota(jnp.int32, (32, 32), 0)
     eye = sub32 == lax.broadcasted_iota(jnp.int32, (32, 32), 1)
     dev_f = jnp.broadcast_to(dev_of.astype(F32), (32, 32))
     dev_col = jnp.sum(jnp.where(eye, dev_f, 0.0), axis=1, keepdims=True)
     hot_t = lax.broadcasted_iota(jnp.int32, (32, 64), 1).astype(F32) == jnp.broadcast_to(dev_col, (32, 64))
+    pack_fluid(1, [j for j in range(20) if j != 4])
+    for x in range(1, 4):
+        sink[x] = jnp.zeros((32, 128), F32)
+    wait_all(rwb.at[0:7], b2_s, b2_r, near_b).wait_recv()
     seen = jnp.concatenate([rwb[b] for b in range(8)], axis=0)
     wall_seen = jnp.dot(
         hot_t.astype(F32), seen, precision=lax.Precision.HIGHEST, preferred_element_type=F32
     )
-    heat_flux = p_ref[0] / rho_ref[0] - wall_seen
+    heat_flux = face_temp - wall_seen
     sink[0] = heat_flux
-    for x in range(1, 4):
-        sink[x] = jnp.zeros((32, 128), F32)
     us[1, 4, 1, 8:40, :] = us[1, 4, 1, 8:40, :] - DT * heat_flux
     halo[1][2].start()
-    pack_fluid(1)
+    pack_fluid(1, (4,), True)
     for c in halo[1][3:]:
         c.start()
     own_prims(1)

time: 41.7 us -> 41.5 us (level)
  no operation moved by 1% of the time
where the time goes in v4:
time: 41.5 us; the launch traced here: 41.3 us
  Pallas kernels  38.4 us (93%)
  local copies, waits for them, and re-layouts  2.35 us (6%)
  between operations  0.65 us (2%)
    pallas_call x1, Pallas kernels, shards(): pl.pallas_call(kernel, out_shape=(jax.ShapeDtypeStruct((5, 4, 32, 128), F...  38.4 us
    unnamed x4, local copies, waits for them, and re-layouts  2.35 us

profile of v4, /device:TPU:1, one launch (start us, length us, event | category | flops | bytes accessed | tf_op | source)
XLA Modules:
  0.0 41.3 jit_solution(30369863828255731)
XLA Ops:
  0.6 38.4 %shard_map.95 = (f32[5,4,32,128]{3,2,1,0:T(8,128)}, f32[8,8,128]{2,1,0:T(8,128)}) custom-call(f32[4,32,128]{2,1,0:T(8,128)} %rho_hbm.1, f32[3,4,32,128]{3,2,1,0:T(8,128)} %vel_hbm.1, f32[4,32,128]{2,1,0:T(8,128)} %p_hbm.1, s32[1,1,32]{2,1,0:T(1,128)} %idx_hbm.1, f32[8,8,128]{2,1,0:T(8,128)} %x0_hbm.1, f32[6,8,8,128]{3,2,1,0:T(8,128)} %fc_hbm.1, ...), custom_call_target="tpu_custom_call" | custom-call | tf_op jit(solution)/shard_map/pallas_call | solution.py:556
  39.0 0.0 copy-start
  39.0 1.7 %copy.12 = f32[5,4,32,128]{3,2,1,0:T(8,128)} copy(f32[5,4,32,128]{3,2,1,0:T(8,128)} %get-tuple-element.4) | data formatting | bytes 655360
  40.7 0.0 copy-done
  40.7 0.6 %copy.13 = f32[8,8,128]{2,1,0:T(8,128)} copy(f32[8,8,128]{2,1,0:T(8,128)S(1)} %copy-done) | data formatting | bytes 65536
Async XLA Ops:
  39.0 1.7 %copy-start = (f32[8,8,128]{2,1,0:T(8,128)S(1)}, f32[8,8,128]{2,1,0:T(8,128)}, u32[]{:S(2)}) copy-start(f32[8,8,128]{2,1,0:T(8,128)} %get-tuple-element.5) | copy-start | bytes 98308
